TPU v7x, 512 devices: a whole 4x8x8 slice. The times are simulated.
512 devices in a mesh: dom: 512 (over x, y, z, core).
Axes of the slice: x: 4, y: 8, z: 8, core: 2. Of those that a mesh axis runs over, the one named last changes fastest.
Arguments:
- positions: float32 [32768, 3, 128], P('dom'), may hold values from -2 to 2, as said below
- moments: float32 [32768, 3, 128], P('dom'), may hold values from -1 to 1
- fwd_cells: int32 [512, 9, 64], P('dom'), may hold values from 0 to 583, as said below
- fwd_leaves: int32 [512, 9, 20], P('dom'), may hold values from 0 to 223, as said below
- fwd_counts: int32 [512, 9, 2], P('dom'), may hold values from 5 to 64, as said below
- cell_list: int32 [32768, 64], P('dom'), may hold values from 0 to 647, as said below
- cell_len: int32 [32768], P('dom'), may hold values from 1 to 64, as said below
- leaf_list: int32 [32768, 8], P('dom'), may hold values from 0 to 243, as said below
- leaf_len: int32 [32768], P('dom'), may hold values from 1 to 8, as said below
Outputs:
- field: float32 [32768, 3, 128], P('dom')
Inputs may be any that keep to these rules, and one draw needn't show every extreme that they name: `fwd_cells`: section b entries are slots that already exist in the sender's pool before section b: below 72 + b * 64. `fwd_leaves`: section b entries lie below 64 + b * 20. `fwd_counts`: column 0 counts cells, from 64 // 4 (at least 1) to 64; column 1 counts leaf blocks, from 20 // 4 (at least 1) to 20; every domain sends a full buffer of both at some section. `cell_list`: slots of the final cell pool; some may be empty (zero) slots. `cell_len`: every domain has a leaf with exactly 64 entries; a domain's mean length may be up to three times another's. `leaf_list`: entry 0 of a leaf's list is the leaf itself and entry 1 one of the 8 leaves under its parent cell; the other entries are slots of the final leaf pool, some of which may be empty (zero) slots. `leaf_len`: every domain has a leaf with exactly 8 entries; a domain's mean length may be up to three times another's. `positions`: each leaf's particles scatter around a centre of their own; the centres of a domain's leaves fill a compact region of space.
All inputs are finite; a program needn't handle non-finite values.
Results may differ from a plain program's by a relative error of at most 0.0003.
Values sent between devices are 32-bit elements; how exact they have to be, the bound alone decides.
A program may use at most 128 MiB of HBM per device.

v0:
```python
import jax
import jax.numpy as jnp
from jax import lax
from jax.sharding import PartitionSpec as P

SOFT = 1.0
DEMAG = 4.1887902047863905
BLOCK = 16


def from_partner(block, axis, stride):
    count = lax.axis_size(axis)
    route = []
    for low in range(count):
        high = low | 1 << stride
        if high != low and high < count:
            route += [(low, high), (high, low)]
    return lax.ppermute(block, axis, route)


def leaf_cells(pos, mom):
    center = jnp.mean(pos, axis=2)
    offset = pos - center[:, :, None]
    total = jnp.sum(mom, axis=2)
    second = jnp.sum(offset[:, :, None, :] * mom[:, None, :, :], axis=3)
    return (center, total, second)


def parent_cells(center, total, second):
    kids_c = center.reshape(-1, 8, 3)
    kids_t = total.reshape(-1, 8, 3)
    kids_s = second.reshape(-1, 8, 3, 3)
    pc = jnp.mean(kids_c, axis=1)
    pt = jnp.sum(kids_t, axis=1)
    shift = kids_c - pc[:, None, :]
    ps = jnp.sum(kids_s + shift[:, :, :, None] * kids_t[:, :, None, :], axis=1)
    return (pc, pt, ps)


def pack_columns(center, total, second):
    return jnp.concatenate([center.T, total.T, second.reshape(-1, 9).T], axis=0)


def pair_field(targets, block):
    src = block[:, 0:3]
    mom = block[:, 3:6]
    sep = targets[:, :, :, None] - src[:, :, None, :]
    quad = jnp.sum(sep * sep, axis=1) + SOFT
    inv = lax.rsqrt(quad)
    inv3 = inv * inv * inv
    inv5 = inv3 / quad
    along = jnp.sum(mom[:, :, None, :] * sep, axis=1)
    term = 3.0 * sep * (along * inv5)[:, None] - mom[:, :, None, :] * inv3[:, None]
    return jnp.sum(term, axis=3)


def cell_field(targets, cells):
    center = cells[0:3][..., None]
    total = cells[3:6][..., None]
    second = cells[6:15].reshape((3, 3) + cells.shape[1:])[..., None]
    sep = jnp.transpose(targets, (1, 0, 2))[:, :, None, :] - center
    quad = jnp.sum(sep * sep, axis=0) + SOFT
    inv = lax.rsqrt(quad)
    inv3 = inv * inv * inv
    inv5 = inv3 / quad
    inv7 = inv5 / quad
    along = jnp.sum(total * sep, axis=0)
    qsep = jnp.sum(second * sep[None], axis=1)
    qtsep = jnp.sum(second * sep[:, None], axis=0)
    trace = second[0, 0] + second[1, 1] + second[2, 2]
    rqr = jnp.sum(sep * qsep, axis=0)
    return (
        3.0 * sep * (along * inv5)
        - total * inv3
        - 3.0 * inv5 * (qsep + sep * trace + qtsep)
        + 15.0 * inv7 * sep * rqr
    )


def leaf_pass(targets, pool_leaves, lists, lower, upper, acc):

    def leaf_step(k, acc):
        ids = lists[:, k]
        blk = jnp.take(pool_leaves, ids, axis=0)
        keep = (k >= lower) & (k < upper)
        return acc + jnp.where(keep[:, None, None], pair_field(targets, blk), 0.0)

    return lax.fori_loop(jnp.min(lower), jnp.max(upper), leaf_step, acc)


def cell_pass(targets, pool_cells, lists, lower, upper, acc):

    def cell_step(j, acc):
        ids = lax.dynamic_slice_in_dim(lists, j * BLOCK, BLOCK, 1)
        cells = jnp.take(pool_cells, ids, axis=1)
        part = cell_field(targets, cells)
        slot = j * BLOCK + jnp.arange(BLOCK, dtype=jnp.int32)
        keep = (slot[None, :] >= lower[:, None]) & (slot[None, :] < upper[:, None])
        summed = jnp.sum(jnp.where(keep[None, :, :, None], part, 0.0), axis=2)
        return acc + jnp.transpose(summed, (1, 0, 2))

    first = jnp.min(lower) // BLOCK
    last = (jnp.max(upper) + BLOCK - 1) // BLOCK
    return lax.fori_loop(first, last, cell_step, acc)


def per_device(
    positions, moments, fwd_cells, fwd_leaves, fwd_counts, cell_list, cell_len, leaf_list, leaf_len
):
    leaves = positions.shape[0]
    width = positions.shape[2]
    domains = lax.axis_size("dom")
    sections = domains.bit_length() - 1
    cell_sends = fwd_cells.shape[2]
    leaf_sends = fwd_leaves.shape[2]
    own_count = leaves + leaves // 8
    moment_sum = lax.psum(jnp.sum(moments, axis=(0, 2)), "dom")
    uniform = -DEMAG * moment_sum / (domains * leaves)
    center, total, second = leaf_cells(positions, moments)
    pc, pt, ps = parent_cells(center, total, second)
    own_cells = jnp.concatenate(
        [pack_columns(center, total, second), pack_columns(pc, pt, ps)], axis=1
    )
    blocks = jnp.concatenate([positions, moments], axis=1)
    pool_leaves = jnp.concatenate(
        [blocks, jnp.zeros((sections * leaf_sends, 6, width), jnp.float32)], axis=0
    )
    pool_cells = jnp.concatenate(
        [own_cells, jnp.zeros((15, sections * cell_sends), jnp.float32)], axis=1
    )
    field = jnp.zeros(positions.shape, jnp.float32)
    for section in range(sections):
        counts = fwd_counts[0, section]
        leaf_pick = jnp.take(pool_leaves, fwd_leaves[0, section], axis=0)
        leaf_live = jnp.arange(leaf_sends, dtype=jnp.int32) < counts[1]
        leaf_pick = jnp.where(leaf_live[:, None, None], leaf_pick, 0.0)
        cell_pick = jnp.take(pool_cells, fwd_cells[0, section], axis=1)
        cell_pick = jnp.where(
            jnp.arange(cell_sends, dtype=jnp.int32)[None, :] < counts[0], cell_pick, 0.0
        )
        got_cells, got_leaves = from_partner((cell_pick, leaf_pick), "dom", section)
        pool_cells = lax.dynamic_update_slice_in_dim(
            pool_cells, got_cells, own_count + section * cell_sends, 1
        )
        pool_leaves = lax.dynamic_update_slice_in_dim(
            pool_leaves, got_leaves, leaves + section * leaf_sends, 0
        )
    start = jnp.zeros_like(leaf_len)
    field = leaf_pass(positions, pool_leaves, leaf_list, start, leaf_len, field)
    field = cell_pass(positions, pool_cells, cell_list, start, cell_len, field)
    return field + uniform[None, :, None]


def solution(mesh):
    in_specs = (
        P("dom", None, None),
        P("dom", None, None),
        P("dom", None, None),
        P("dom", None, None),
        P("dom", None, None),
        P("dom", None),
        P("dom"),
        P("dom", None),
        P("dom"),
    )
    out_specs = P("dom", None, None)
    return jax.shard_map(
        per_device, mesh=mesh, in_specs=in_specs, out_specs=out_specs, check_vma=False
    )
```

profile of v0, /device:TPU:6, one launch (start us, length us, event | category | flops | bytes accessed | tf_op | source)
XLA Modules:
  0.0 462.0 jit_solution(15016459273644455395)
XLA Ops:
  22.4 103.6 %psum.7 = f32[3]{0:T(128)S(1)} all-reduce(f32[3]{0:T(128)S(1)} %get-tuple-element.120), channel_id=1, replica_groups=mesh['dom'=512] {'dom'}, use_global_device_ids=true, to_apply=%region_22.25 | all-reduce | flops 3 | bytes 24 | tf_op jit(solution)/shard_map/psum | solution.py:117
  145.8 5.7 %collective-permute-done.12 = f32[15,64]{0,1:T(8,128)S(1)} collective-permute-done((f32[15,64]{0,1:T(8,128)S(1)}, f32[15,64]{0,1:T(8,128)S(1)}, u32[]{:S(2)}, u32[]{:S(2)}) %collective-permute-start.12) | collective-permute-done | bytes 3872 | tf_op jit(solution)/shard_map/ppermute | solution.py:18
  177.9 5.8 %collective-permute-start.15 = (f32[15,64]{0,1:T(8,128)S(1)}, f32[15,64]{0,1:T(8,128)S(1)}, u32[]{:S(2)}, u32[]{:S(2)}) collective-permute-start(f32[15,64]{0,1:T(8,128)S(1)} %bitcast_select_fusion.2), channel_id=1, source_target_pairs={{0,64},{64,0},{1,65},{65,1},{2,66},{66,2},{3,67},{67,3},{4,68},{68... | collective-permute-start | bytes 11528 | tf_op jit(solution)/shard_map/ppermute | solution.py:18
  206.3 8.5 %collective-permute-done.6 = f32[20,6,128]{2,1,0:T(8,128)S(1)} collective-permute-done((f32[20,6,128]{2,1,0:T(8,128)S(1)}, f32[20,6,128]{2,1,0:T(8,128)S(1)}, u32[]{:S(2)}, u32[]{:S(2)}) %collective-permute-start.6) | collective-permute-done | bytes 61472 | tf_op jit(solution)/shard_map/ppermute | solution.py:18
  217.7 5.8 %collective-permute-start.17 = (f32[15,64]{0,1:T(8,128)S(1)}, f32[15,64]{0,1:T(8,128)S(1)}, u32[]{:S(2)}, u32[]{:S(2)}) collective-permute-start(f32[15,64]{0,1:T(8,128)S(1)} %bitcast_select_fusion), channel_id=1, source_target_pairs={{0,256},{256,0},{1,257},{257,1},{2,258},{258,2},{3,259},{259,3},{4... | collective-permute-start | bytes 11528 | tf_op jit(solution)/shard_map/ppermute | solution.py:18
  226.7 5.4 %collective-permute-done.8 = f32[20,6,128]{2,1,0:T(8,128)S(1)} collective-permute-done((f32[20,6,128]{2,1,0:T(8,128)S(1)}, f32[20,6,128]{2,1,0:T(8,128)S(1)}, u32[]{:S(2)}, u32[]{:S(2)}) %collective-permute-start.8) | collective-permute-done | bytes 61472 | tf_op jit(solution)/shard_map/ppermute | solution.py:18
  232.1 136.0 %while.20 = (s32[]{:T(128)}, f32[64,3,128]{2,1,0:T(4,128)S(1)}, s32[]{:T(128)}, s32[64]{0:T(128)S(1)}, f32[64,3,128]{2,1,0:T(4,128)S(1)}, /*index=5*/s32[64,8]{0...) while((s32[]{:T(128)}, f32[64,3,128]{2,1,0:T(4,128)S(1)}, s32[]{:T(128)}, ...), condition=%wide.region_5.7_spmd, body=%wide.region_1.6_spmd.sunk | while | flops 35726852 | bytes 35722908 | solution.py:88
  234.3 4.7 %fusion.31 = (f32[64,128,128]{2,1,0:T(8,128)S(1)}, f32[64,128,128]{2,1,0:T(8,128)S(1)}) fusion(f32[64,3,128]{2,1,0:T(4,128)S(1)} %get-tuple-element.360, f32[64,3,128]{2,1,0:T(4,128)S(1)} %get-tuple-element.361, f32[64,3,128]{2,1,0:T(4,128)S(1)} %get-tuple-element.410), kind=kLoop, calls=%fused_computation.23.clone.1 | loop fusion | flops 13631488 | bytes 8683520 | tf_op jit(solution)/shard_map/while/body/reduce_sum | solution.py:52
  241.0 7.7 %fusion.32 = f32[64,3,128]{2,1,0:T(4,128)S(1)} fusion(f32[64,128,128]{2,1,0:T(8,128)S(1)} %get-tuple-element.364, f32[64,128,128]{2,1,0:T(8,128)S(1)} %get-tuple-element.365, f32[64,3,128]{2,1,0:T(4,128)S(1)} %get-tuple-element.360, f32[64,3,128]{2,1,0:T(4,128)S(1)} %get-tuple-element.361, f32[64,3,128]{2,1,0:T(4,128)S(1)} %get-tuple-element.410), kind=kLoop, calls=%fused_computation.26.clone.1 | loop fusion | flops 15704064 | bytes 8781824 | tf_op jit(solution)/shard_map/while/body/reduce_sum | solution.py:54
  251.3 4.7 %fusion.31 = (f32[64,128,128]{2,1,0:T(8,128)S(1)}, f32[64,128,128]{2,1,0:T(8,128)S(1)}) fusion(f32[64,3,128]{2,1,0:T(4,128)S(1)} %get-tuple-element.360, f32[64,3,128]{2,1,0:T(4,128)S(1)} %get-tuple-element.361, f32[64,3,128]{2,1,0:T(4,128)S(1)} %get-tuple-element.410), kind=kLoop, calls=%fused_computation.23.clone.1 | loop fusion | flops 13631488 | bytes 8683520 | tf_op jit(solution)/shard_map/while/body/reduce_sum | solution.py:52
  257.9 7.7 %fusion.32 = f32[64,3,128]{2,1,0:T(4,128)S(1)} fusion(f32[64,128,128]{2,1,0:T(8,128)S(1)} %get-tuple-element.364, f32[64,128,128]{2,1,0:T(8,128)S(1)} %get-tuple-element.365, f32[64,3,128]{2,1,0:T(4,128)S(1)} %get-tuple-element.360, f32[64,3,128]{2,1,0:T(4,128)S(1)} %get-tuple-element.361, f32[64,3,128]{2,1,0:T(4,128)S(1)} %get-tuple-element.410), kind=kLoop, calls=%fused_computation.26.clone.1 | loop fusion | flops 15704064 | bytes 8781824 | tf_op jit(solution)/shard_map/while/body/reduce_sum | solution.py:54
  268.2 4.7 %fusion.31 = (f32[64,128,128]{2,1,0:T(8,128)S(1)}, f32[64,128,128]{2,1,0:T(8,128)S(1)}) fusion(f32[64,3,128]{2,1,0:T(4,128)S(1)} %get-tuple-element.360, f32[64,3,128]{2,1,0:T(4,128)S(1)} %get-tuple-element.361, f32[64,3,128]{2,1,0:T(4,128)S(1)} %get-tuple-element.410), kind=kLoop, calls=%fused_computation.23.clone.1 | loop fusion | flops 13631488 | bytes 8683520 | tf_op jit(solution)/shard_map/while/body/reduce_sum | solution.py:52
  274.8 7.7 %fusion.32 = f32[64,3,128]{2,1,0:T(4,128)S(1)} fusion(f32[64,128,128]{2,1,0:T(8,128)S(1)} %get-tuple-element.364, f32[64,128,128]{2,1,0:T(8,128)S(1)} %get-tuple-element.365, f32[64,3,128]{2,1,0:T(4,128)S(1)} %get-tuple-element.360, f32[64,3,128]{2,1,0:T(4,128)S(1)} %get-tuple-element.361, f32[64,3,128]{2,1,0:T(4,128)S(1)} %get-tuple-element.410), kind=kLoop, calls=%fused_computation.26.clone.1 | loop fusion | flops 15704064 | bytes 8781824 | tf_op jit(solution)/shard_map/while/body/reduce_sum | solution.py:54
  285.1 4.7 %fusion.31 = (f32[64,128,128]{2,1,0:T(8,128)S(1)}, f32[64,128,128]{2,1,0:T(8,128)S(1)}) fusion(f32[64,3,128]{2,1,0:T(4,128)S(1)} %get-tuple-element.360, f32[64,3,128]{2,1,0:T(4,128)S(1)} %get-tuple-element.361, f32[64,3,128]{2,1,0:T(4,128)S(1)} %get-tuple-element.410), kind=kLoop, calls=%fused_computation.23.clone.1 | loop fusion | flops 13631488 | bytes 8683520 | tf_op jit(solution)/shard_map/while/body/reduce_sum | solution.py:52
  291.8 7.7 %fusion.32 = f32[64,3,128]{2,1,0:T(4,128)S(1)} fusion(f32[64,128,128]{2,1,0:T(8,128)S(1)} %get-tuple-element.364, f32[64,128,128]{2,1,0:T(8,128)S(1)} %get-tuple-element.365, f32[64,3,128]{2,1,0:T(4,128)S(1)} %get-tuple-element.360, f32[64,3,128]{2,1,0:T(4,128)S(1)} %get-tuple-element.361, f32[64,3,128]{2,1,0:T(4,128)S(1)} %get-tuple-element.410), kind=kLoop, calls=%fused_computation.26.clone.1 | loop fusion | flops 15704064 | bytes 8781824 | tf_op jit(solution)/shard_map/while/body/reduce_sum | solution.py:54
  302.0 4.7 %fusion.31 = (f32[64,128,128]{2,1,0:T(8,128)S(1)}, f32[64,128,128]{2,1,0:T(8,128)S(1)}) fusion(f32[64,3,128]{2,1,0:T(4,128)S(1)} %get-tuple-element.360, f32[64,3,128]{2,1,0:T(4,128)S(1)} %get-tuple-element.361, f32[64,3,128]{2,1,0:T(4,128)S(1)} %get-tuple-element.410), kind=kLoop, calls=%fused_computation.23.clone.1 | loop fusion | flops 13631488 | bytes 8683520 | tf_op jit(solution)/shard_map/while/body/reduce_sum | solution.py:52
  308.7 7.7 %fusion.32 = f32[64,3,128]{2,1,0:T(4,128)S(1)} fusion(f32[64,128,128]{2,1,0:T(8,128)S(1)} %get-tuple-element.364, f32[64,128,128]{2,1,0:T(8,128)S(1)} %get-tuple-element.365, f32[64,3,128]{2,1,0:T(4,128)S(1)} %get-tuple-element.360, f32[64,3,128]{2,1,0:T(4,128)S(1)} %get-tuple-element.361, f32[64,3,128]{2,1,0:T(4,128)S(1)} %get-tuple-element.410), kind=kLoop, calls=%fused_computation.26.clone.1 | loop fusion | flops 15704064 | bytes 8781824 | tf_op jit(solution)/shard_map/while/body/reduce_sum | solution.py:54
  318.9 4.7 %fusion.31 = (f32[64,128,128]{2,1,0:T(8,128)S(1)}, f32[64,128,128]{2,1,0:T(8,128)S(1)}) fusion(f32[64,3,128]{2,1,0:T(4,128)S(1)} %get-tuple-element.360, f32[64,3,128]{2,1,0:T(4,128)S(1)} %get-tuple-element.361, f32[64,3,128]{2,1,0:T(4,128)S(1)} %get-tuple-element.410), kind=kLoop, calls=%fused_computation.23.clone.1 | loop fusion | flops 13631488 | bytes 8683520 | tf_op jit(solution)/shard_map/while/body/reduce_sum | solution.py:52
  325.6 7.7 %fusion.32 = f32[64,3,128]{2,1,0:T(4,128)S(1)} fusion(f32[64,128,128]{2,1,0:T(8,128)S(1)} %get-tuple-element.364, f32[64,128,128]{2,1,0:T(8,128)S(1)} %get-tuple-element.365, f32[64,3,128]{2,1,0:T(4,128)S(1)} %get-tuple-element.360, f32[64,3,128]{2,1,0:T(4,128)S(1)} %get-tuple-element.361, f32[64,3,128]{2,1,0:T(4,128)S(1)} %get-tuple-element.410), kind=kLoop, calls=%fused_computation.26.clone.1 | loop fusion | flops 15704064 | bytes 8781824 | tf_op jit(solution)/shard_map/while/body/reduce_sum | solution.py:54
  335.8 4.7 %fusion.31 = (f32[64,128,128]{2,1,0:T(8,128)S(1)}, f32[64,128,128]{2,1,0:T(8,128)S(1)}) fusion(f32[64,3,128]{2,1,0:T(4,128)S(1)} %get-tuple-element.360, f32[64,3,128]{2,1,0:T(4,128)S(1)} %get-tuple-element.361, f32[64,3,128]{2,1,0:T(4,128)S(1)} %get-tuple-element.410), kind=kLoop, calls=%fused_computation.23.clone.1 | loop fusion | flops 13631488 | bytes 8683520 | tf_op jit(solution)/shard_map/while/body/reduce_sum | solution.py:52
  342.5 7.7 %fusion.32 = f32[64,3,128]{2,1,0:T(4,128)S(1)} fusion(f32[64,128,128]{2,1,0:T(8,128)S(1)} %get-tuple-element.364, f32[64,128,128]{2,1,0:T(8,128)S(1)} %get-tuple-element.365, f32[64,3,128]{2,1,0:T(4,128)S(1)} %get-tuple-element.360, f32[64,3,128]{2,1,0:T(4,128)S(1)} %get-tuple-element.361, f32[64,3,128]{2,1,0:T(4,128)S(1)} %get-tuple-element.410), kind=kLoop, calls=%fused_computation.26.clone.1 | loop fusion | flops 15704064 | bytes 8781824 | tf_op jit(solution)/shard_map/while/body/reduce_sum | solution.py:54
  352.7 4.7 %fusion.31 = (f32[64,128,128]{2,1,0:T(8,128)S(1)}, f32[64,128,128]{2,1,0:T(8,128)S(1)}) fusion(f32[64,3,128]{2,1,0:T(4,128)S(1)} %get-tuple-element.360, f32[64,3,128]{2,1,0:T(4,128)S(1)} %get-tuple-element.361, f32[64,3,128]{2,1,0:T(4,128)S(1)} %get-tuple-element.410), kind=kLoop, calls=%fused_computation.23.clone.1 | loop fusion | flops 13631488 | bytes 8683520 | tf_op jit(solution)/shard_map/while/body/reduce_sum | solution.py:52
  359.4 7.7 %fusion.32 = f32[64,3,128]{2,1,0:T(4,128)S(1)} fusion(f32[64,128,128]{2,1,0:T(8,128)S(1)} %get-tuple-element.364, f32[64,128,128]{2,1,0:T(8,128)S(1)} %get-tuple-element.365, f32[64,3,128]{2,1,0:T(4,128)S(1)} %get-tuple-element.360, f32[64,3,128]{2,1,0:T(4,128)S(1)} %get-tuple-element.361, f32[64,3,128]{2,1,0:T(4,128)S(1)} %get-tuple-element.410), kind=kLoop, calls=%fused_computation.26.clone.1 | loop fusion | flops 15704064 | bytes 8781824 | tf_op jit(solution)/shard_map/while/body/reduce_sum | solution.py:54
  368.7 91.6 %while.21 = (s32[]{:T(128)}, f32[64,3,128]{2,0,1:T(8,128)}, s32[]{:T(128)}, s32[64]{0:T(128)S(1)}, f32[64,3,128]{2,0,1:T(8,128)}, /*index=5*/s32[64,64]{1,0:T(8,...) while((s32[]{:T(128)}, f32[64,3,128]{2,0,1:T(8,128)}, s32[]{:T(128)}, ...), condition=%wide.region_20.23_spmd, body=%wide.region_13.22_spmd.sunk | while | flops 13527094 | bytes 26993372 | solution.py:104
  (358 shorter events, 218.9 us)
Async XLA Ops:
  0.0 8.2 %copy-start.5 = (f32[64,3,128]{2,0,1:T(8,128)S(1)}, f32[64,3,128]{2,0,1:T(8,128)}, u32[]{:S(2)}) copy-start(f32[64,3,128]{2,0,1:T(8,128)} %param.18) | copy-start | bytes 294916
  1.0 10.5 %copy-start.8 = (s32[1,9,64]{2,0,1:T(1,128)S(1)}, s32[1,9,64]{2,0,1:T(1,128)}, u32[]{:S(2)}) copy-start(s32[1,9,64]{2,0,1:T(1,128)} %param.19) | copy-start | bytes 6916
  5.6 150.0 %copy-start.6 = (s32[64]{0:T(128)S(1)}, s32[64]{0:T(128)}, u32[]{:S(2)}) copy-start(s32[64]{0:T(128)} %param.23) | copy-start | bytes 772
  5.6 151.4 %copy-start.7 = (s32[64]{0:T(128)S(1)}, s32[64]{0:T(128)}, u32[]{:S(2)}) copy-start(s32[64]{0:T(128)} %param.25) | copy-start | bytes 772
  6.3 152.3 %collective-permute-start = (f32[20,6,128]{2,1,0:T(8,128)S(1)}, f32[20,6,128]{2,1,0:T(8,128)S(1)}, u32[]{:S(2)}, u32[]{:S(2)}) collective-permute-start(f32[20,6,128]{2,1,0:T(8,128)S(1)} %select_select_fusion.8), channel_id=1, source_target_pairs={{0,1},{1,0},{2,3},{3,2},{4,5},{5,4},{6,7},{7,6},{8,9},{9,8},{10,11... | collective-permute-start | bytes 184328 | tf_op jit(solution)/shard_map/ppermute | solution.py:18
  12.9 114.3 %collective-permute-start.9 = (f32[15,64]{0,1:T(8,128)S(1)}, f32[15,64]{0,1:T(8,128)S(1)}, u32[]{:S(2)}, u32[]{:S(2)}) collective-permute-start(f32[15,64]{0,1:T(8,128)S(1)} %bitcast_select_fusion.8), channel_id=1, source_target_pairs={{0,1},{1,0},{2,3},{3,2},{4,5},{5,4},{6,7},{7,6},{8,9},{9,8},{10,11... | collective-permute-start | bytes 11528 | tf_op jit(solution)/shard_map/ppermute | solution.py:18
  127.9 5.8 %collective-permute-start.10 = (f32[15,64]{0,1:T(8,128)S(1)}, f32[15,64]{0,1:T(8,128)S(1)}, u32[]{:S(2)}, u32[]{:S(2)}) collective-permute-start(f32[15,64]{0,1:T(8,128)S(1)} %bitcast_select_fusion.7), channel_id=1, source_target_pairs={{0,2},{2,0},{1,3},{3,1},{4,6},{6,4},{5,7},{7,5},{8,10},{10,8},{9,1... | collective-permute-start | bytes 11528 | tf_op jit(solution)/shard_map/ppermute | solution.py:18
  134.4 6.7 %collective-permute-start.11 = (f32[15,64]{0,1:T(8,128)S(1)}, f32[15,64]{0,1:T(8,128)S(1)}, u32[]{:S(2)}, u32[]{:S(2)}) collective-permute-start(f32[15,64]{0,1:T(8,128)S(1)} %bitcast_select_fusion.6), channel_id=1, source_target_pairs={{0,4},{4,0},{1,5},{5,1},{2,6},{6,2},{3,7},{7,3},{8,12},{12,8},{9,1... | collective-permute-start | bytes 11528 | tf_op jit(solution)/shard_map/ppermute | solution.py:18
  141.8 9.7 %collective-permute-start.12 = (f32[15,64]{0,1:T(8,128)S(1)}, f32[15,64]{0,1:T(8,128)S(1)}, u32[]{:S(2)}, u32[]{:S(2)}) collective-permute-start(f32[15,64]{0,1:T(8,128)S(1)} %bitcast_select_fusion.5), channel_id=1, source_target_pairs={{0,8},{8,0},{1,9},{9,1},{2,10},{10,2},{3,11},{11,3},{4,12},{12,4},... | collective-permute-start | bytes 11528 | tf_op jit(solution)/shard_map/ppermute | solution.py:18
  152.2 5.8 %collective-permute-start.13 = (f32[15,64]{0,1:T(8,128)S(1)}, f32[15,64]{0,1:T(8,128)S(1)}, u32[]{:S(2)}, u32[]{:S(2)}) collective-permute-start(f32[15,64]{0,1:T(8,128)S(1)} %bitcast_select_fusion.4), channel_id=1, source_target_pairs={{0,16},{16,0},{1,17},{17,1},{2,18},{18,2},{3,19},{19,3},{4,20},{20... | collective-permute-start | bytes 11528 | tf_op jit(solution)/shard_map/ppermute | solution.py:18
  159.3 6.7 %collective-permute-start.1 = (f32[20,6,128]{2,1,0:T(8,128)S(1)}, f32[20,6,128]{2,1,0:T(8,128)S(1)}, u32[]{:S(2)}, u32[]{:S(2)}) collective-permute-start(f32[20,6,128]{2,1,0:T(8,128)S(1)} %select_select_fusion.7), channel_id=1, source_target_pairs={{0,2},{2,0},{1,3},{3,1},{4,6},{6,4},{5,7},{7,5},{8,10},{10,8},{9,1... | collective-permute-start | bytes 184328 | tf_op jit(solution)/shard_map/ppermute | solution.py:18
  161.5 7.4 %collective-permute-start.14 = (f32[15,64]{0,1:T(8,128)S(1)}, f32[15,64]{0,1:T(8,128)S(1)}, u32[]{:S(2)}, u32[]{:S(2)}) collective-permute-start(f32[15,64]{0,1:T(8,128)S(1)} %bitcast_select_fusion.3), channel_id=1, source_target_pairs={{0,32},{32,0},{1,33},{33,1},{2,34},{34,2},{3,35},{35,3},{4,36},{36... | collective-permute-start | bytes 11528 | tf_op jit(solution)/shard_map/ppermute | solution.py:18
  166.7 7.2 %collective-permute-start.2 = (f32[20,6,128]{2,1,0:T(8,128)S(1)}, f32[20,6,128]{2,1,0:T(8,128)S(1)}, u32[]{:S(2)}, u32[]{:S(2)}) collective-permute-start(f32[20,6,128]{2,1,0:T(8,128)S(1)} %select_select_fusion.6), channel_id=1, source_target_pairs={{0,4},{4,0},{1,5},{5,1},{2,6},{6,2},{3,7},{7,3},{8,12},{12,8},{9,1... | collective-permute-start | bytes 184328 | tf_op jit(solution)/shard_map/ppermute | solution.py:18
  174.7 10.2 %collective-permute-start.3 = (f32[20,6,128]{2,1,0:T(8,128)S(1)}, f32[20,6,128]{2,1,0:T(8,128)S(1)}, u32[]{:S(2)}, u32[]{:S(2)}) collective-permute-start(f32[20,6,128]{2,1,0:T(8,128)S(1)} %select_select_fusion.5), channel_id=1, source_target_pairs={{0,8},{8,0},{1,9},{9,1},{2,10},{10,2},{3,11},{11,3},{4,12},{12,4},... | collective-permute-start | bytes 184328 | tf_op jit(solution)/shard_map/ppermute | solution.py:18
  177.9 10.6 %collective-permute-start.15 = (f32[15,64]{0,1:T(8,128)S(1)}, f32[15,64]{0,1:T(8,128)S(1)}, u32[]{:S(2)}, u32[]{:S(2)}) collective-permute-start(f32[15,64]{0,1:T(8,128)S(1)} %bitcast_select_fusion.2), channel_id=1, source_target_pairs={{0,64},{64,0},{1,65},{65,1},{2,66},{66,2},{3,67},{67,3},{4,68},{68... | collective-permute-start | bytes 11528 | tf_op jit(solution)/shard_map/ppermute | solution.py:18
  185.6 7.2 %collective-permute-start.4 = (f32[20,6,128]{2,1,0:T(8,128)S(1)}, f32[20,6,128]{2,1,0:T(8,128)S(1)}, u32[]{:S(2)}, u32[]{:S(2)}) collective-permute-start(f32[20,6,128]{2,1,0:T(8,128)S(1)} %select_select_fusion.4), channel_id=1, source_target_pairs={{0,16},{16,0},{1,17},{17,1},{2,18},{18,2},{3,19},{19,3},{4,20},{20... | collective-permute-start | bytes 184328 | tf_op jit(solution)/shard_map/ppermute | solution.py:18
  193.5 9.4 %collective-permute-start.5 = (f32[20,6,128]{2,1,0:T(8,128)S(1)}, f32[20,6,128]{2,1,0:T(8,128)S(1)}, u32[]{:S(2)}, u32[]{:S(2)}) collective-permute-start(f32[20,6,128]{2,1,0:T(8,128)S(1)} %select_select_fusion.3), channel_id=1, source_target_pairs={{0,32},{32,0},{1,33},{33,1},{2,34},{34,2},{3,35},{35,3},{4,36},{36... | collective-permute-start | bytes 184328 | tf_op jit(solution)/shard_map/ppermute | solution.py:18
  198.0 7.6 %collective-permute-start.16 = (f32[15,64]{0,1:T(8,128)S(1)}, f32[15,64]{0,1:T(8,128)S(1)}, u32[]{:S(2)}, u32[]{:S(2)}) collective-permute-start(f32[15,64]{0,1:T(8,128)S(1)} %bitcast_select_fusion.1), channel_id=1, source_target_pairs={{0,128},{128,0},{1,129},{129,1},{2,130},{130,2},{3,131},{131,3},{4... | collective-permute-start | bytes 11528 | tf_op jit(solution)/shard_map/ppermute | solution.py:18
  203.6 11.1 %collective-permute-start.6 = (f32[20,6,128]{2,1,0:T(8,128)S(1)}, f32[20,6,128]{2,1,0:T(8,128)S(1)}, u32[]{:S(2)}, u32[]{:S(2)}) collective-permute-start(f32[20,6,128]{2,1,0:T(8,128)S(1)} %select_select_fusion.2), channel_id=1, source_target_pairs={{0,64},{64,0},{1,65},{65,1},{2,66},{66,2},{3,67},{67,3},{4,68},{68... | collective-permute-start | bytes 184328 | tf_op jit(solution)/shard_map/ppermute | solution.py:18
  215.5 8.0 %collective-permute-start.7 = (f32[20,6,128]{2,1,0:T(8,128)S(1)}, f32[20,6,128]{2,1,0:T(8,128)S(1)}, u32[]{:S(2)}, u32[]{:S(2)}) collective-permute-start(f32[20,6,128]{2,1,0:T(8,128)S(1)} %select_select_fusion.1), channel_id=1, source_target_pairs={{0,128},{128,0},{1,129},{129,1},{2,130},{130,2},{3,131},{131,3},{4... | collective-permute-start | bytes 184328 | tf_op jit(solution)/shard_map/ppermute | solution.py:18
  217.7 9.0 %collective-permute-start.17 = (f32[15,64]{0,1:T(8,128)S(1)}, f32[15,64]{0,1:T(8,128)S(1)}, u32[]{:S(2)}, u32[]{:S(2)}) collective-permute-start(f32[15,64]{0,1:T(8,128)S(1)} %bitcast_select_fusion), channel_id=1, source_target_pairs={{0,256},{256,0},{1,257},{257,1},{2,258},{258,2},{3,259},{259,3},{4... | collective-permute-start | bytes 11528 | tf_op jit(solution)/shard_map/ppermute | solution.py:18
  224.2 7.8 %collective-permute-start.8 = (f32[20,6,128]{2,1,0:T(8,128)S(1)}, f32[20,6,128]{2,1,0:T(8,128)S(1)}, u32[]{:S(2)}, u32[]{:S(2)}) collective-permute-start(f32[20,6,128]{2,1,0:T(8,128)S(1)} %select_select_fusion), channel_id=1, source_target_pairs={{0,256},{256,0},{1,257},{257,1},{2,258},{258,2},{3,259},{259,3},{4... | collective-permute-start | bytes 184328 | tf_op jit(solution)/shard_map/ppermute | solution.py:18
  387.1 3.9 copy-start.3
  410.0 3.9 copy-start.3
  (18 other events, 40.0 us)
where the time goes:
time: 465 us; the launch traced here: 462 us
  other arithmetic  206 us (44%)
  blocking collectives  104 us (22%)
  starting transfers between devices  54.7 us (12%)
  local copies, waits for them, and re-layouts  50 us (11%)
  waiting for transfers between devices  38.3 us (8%)
  loops' own time  7.47 us (2%)
    psum x1, blocking collectives, per_device(): moment_sum = lax.psum(jnp.sum(moments, axis=(0, 2)), 'dom')  104 us
    reduce_sum x8, other arithmetic, pair_field(): return jnp.sum(term, axis=3)  61.6 us
    ppermute x18, starting transfers between devices, from_partner(): return lax.ppermute(block, axis, route)  54.7 us
    ppermute x18, waiting for transfers between devices, from_partner(): return lax.ppermute(block, axis, route)  38.3 us
    reduce_sum x8, other arithmetic, pair_field(): along = jnp.sum(mom[:, :, None, :] * sep, axis=1)  37.8 us
    reduce_sum x4, other arithmetic, cell_field(): qsep = jnp.sum(second * sep[None], axis=1)  17.4 us
    reduce_sum x4, other arithmetic, cell_step(): summed = jnp.sum(jnp.where(keep[None, :, :, None], part, 0.0), axis=2)  15.5 us
    mul x8, other arithmetic, pair_field(): 3.0 * sep * (along * inv5)[:, None] - mom[:, :, None, :] * inv3[:, None]  15.5 us
  transfers between devices with their start and end apart: 18, of which 10 were waited for; matrix products, arithmetic and copies ran while one was open for 5% of the time, Pallas kernels for 0%

commit v1 on v0

v1 whole, which is shorter than its diff:
```python
import functools

import jax
import jax.numpy as jnp
from jax import lax
from jax.experimental import pallas as pl
from jax.experimental.pallas import tpu as pltpu
from jax.sharding import PartitionSpec as P

F32 = jnp.float32
BF16 = jnp.bfloat16
DEMAG = 4.1887902047863905
LEAVES = 64
PARENTS = 8
OWN = LEAVES + PARENTS
SECTIONS = 9
CELL_SENDS = 64
LEAF_SENDS = 20
LEAF_POOL = LEAVES + SECTIONS * LEAF_SENDS
CELL_POOL = OWN + SECTIONS * CELL_SENDS
LANES = 128
N_DOM = 512
NEAR_UNROLL = 4
FAR_UNROLL = 4


def iota(shape, dim):
    return lax.broadcasted_iota(jnp.int32, shape, dim)


def pieces(x):
    first = x.astype(BF16).astype(F32)
    rest = x - first
    second = rest.astype(BF16).astype(F32)
    return first, second, rest - second


def far_rows(tile):
    row = lambda k, j: tile[6 + 3 * k + j : 7 + 3 * k + j]
    return jnp.concatenate(
        [
            tile[0:6],
            2.0 * row(0, 0),
            2.0 * row(1, 1),
            2.0 * row(2, 2),
            row(0, 1) + row(1, 0),
            row(0, 2) + row(2, 0),
            row(1, 2) + row(2, 1),
            row(0, 0) + row(1, 1) + row(2, 2),
            jnp.zeros((3, LANES), F32),
        ],
        axis=0,
    )


def own_tile(pos_ref, mom_ref):
    pos = [pos_ref[:, k, :] for k in range(3)]
    mom = [mom_ref[:, k, :] for k in range(3)]
    cen = [jnp.sum(p, axis=1, keepdims=True) * (1.0 / LANES) for p in pos]
    tot = [jnp.sum(m, axis=1, keepdims=True) for m in mom]
    off = [pos[k] - cen[k] for k in range(3)]
    sec = [
        [jnp.sum(off[k] * mom[j], axis=1, keepdims=True) for j in range(3)] for k in range(3)
    ]
    full = lambda x: jnp.broadcast_to(x, (LEAVES, LANES)).reshape(PARENTS, 8, LANES)
    fcen = [full(c) for c in cen]
    ftot = [full(c) for c in tot]
    fsec = [[full(sec[k][j]) for j in range(3)] for k in range(3)]
    pcen = [jnp.sum(c, axis=1, keepdims=True) * 0.125 for c in fcen]
    ptot = [jnp.sum(c, axis=1) for c in ftot]
    psec = [
        [jnp.sum(fsec[k][j] + (fcen[k] - pcen[k]) * ftot[j], axis=1) for j in range(3)]
        for k in range(3)
    ]
    leaf = fcen + ftot + [fsec[k][j] for k in range(3) for j in range(3)]
    up = [c[:, 0, :] for c in pcen] + ptot + [psec[k][j] for k in range(3) for j in range(3)]
    lane = iota((LEAVES, LANES), 1)
    lane_p = iota((PARENTS, LANES), 1)
    rows = jnp.zeros((LEAVES, LANES), F32)
    rows_p = jnp.zeros((PARENTS, LANES), F32)
    for i in range(15):
        rows = jnp.where(lane == i, leaf[i].reshape(LEAVES, LANES), rows)
        rows_p = jnp.where(lane_p == i, up[i], rows_p)
    every = jnp.concatenate([rows, rows_p, jnp.zeros((LANES - OWN, LANES), F32)], axis=0)
    sums = [jnp.sum(p, axis=0, keepdims=True) for p in ptot]
    return jnp.transpose(every)[0:16], sums


def exchange_kernel(
    pos_ref, mom_ref, fl_ref, fn_ref, fc_ref,
    pool_ref, cells_ref, unif_ref,
    split, index, send_l, recv_l, send_c, recv_c, sl_sem, rl_sem, sc_sem, rc_sem,
):
    me = lax.axis_index("dom")
    partners = []
    for b in range(SECTIONS):
        stride = 1 << b
        partners.append(me + (1 - 2 * lax.rem(me // stride, 2)) * stride)
    barrier = pltpu.get_barrier_semaphore()
    for other in partners:
        pl.semaphore_signal(
            barrier, inc=1, device_id=(other,), device_id_type=pl.DeviceIdType.MESH
        )
    pool_ref[0:LEAVES, 0:3, :] = pos_ref[...]
    pool_ref[0:LEAVES, 3:6, :] = mom_ref[...]

    lane16 = iota((16, LANES), 1)
    lane = iota((8, LANES), 1)
    sub = iota((8, LANES), 0)
    index[...] = jnp.full((16, LANES), -1, jnp.int32)
    index[0:SECTIONS, 0:CELL_SENDS] = fc_ref[0]
    raw = index[...]
    past = raw - OWN
    index[...] = jnp.where(
        raw < OWN, raw, LANES + (past // CELL_SENDS) * LANES + lax.rem(past, CELL_SENDS)
    )
    pl.semaphore_wait(barrier, SECTIONS)

    def leaf_copy(b):
        return pltpu.make_async_remote_copy(
            src_ref=send_l.at[b], dst_ref=recv_l.at[b],
            send_sem=sl_sem.at[b], recv_sem=rl_sem.at[b],
            device_id=(partners[b],), device_id_type=pl.DeviceIdType.MESH,
        )

    def cell_copy(b):
        return pltpu.make_async_remote_copy(
            src_ref=send_c.at[b], dst_ref=recv_c.at[b],
            send_sem=sc_sem.at[b], recv_sem=rc_sem.at[b],
            device_id=(partners[b],), device_id_type=pl.DeviceIdType.MESH,
        )

    def send_leaves(b):
        live = fn_ref[0, b, 1]
        for s in range(LEAF_SENDS):
            block = pool_ref[fl_ref[0, b, s]][0:6]
            send_l[b, 6 * s : 6 * s + 6, :] = jnp.where(s < live, block, 0.0)
        leaf_copy(b).start()

    def take_tile(tile, t):
        for i, part in enumerate(pieces(tile)):
            split[16 * i : 16 * i + 16, LANES * t : LANES * t + LANES] = part.astype(BF16)

    def send_cells(b, msum):
        depth = (b + 1) * LANES
        wanted = jnp.where(lane[0:1] < fn_ref[0, b, 0], index[b : b + 1, :], -1)
        hot = jnp.where(iota((depth, LANES), 0) == wanted, 1.0, 0.0).astype(BF16)
        got = jnp.dot(split[:, 0:depth], hot, preferred_element_type=F32)
        got = (got[0:16] + got[16:32]) + got[32:48]
        low = jnp.where(sub == 7, msum, got[8:16])
        send_c[b] = jnp.where(lane < CELL_SENDS, got[0:8], pltpu.roll(low, CELL_SENDS, 1))
        cell_copy(b).start()

    def finish_leaves(first, count):
        part = [pool_ref[first : first + count, i, :] for i in range(6)]
        pool_ref[first : first + count, 6, :] = (
            part[0] * part[0] + part[1] * part[1] + part[2] * part[2]
        )
        pool_ref[first : first + count, 7, :] = (
            part[0] * part[3] + part[1] * part[4] + part[2] * part[5]
        )

    def finish_cells(tile, first, count):
        turned = jnp.transpose(
            jnp.concatenate([far_rows(tile), jnp.zeros((LANES - 16, LANES), F32)], axis=0)
        )
        cells_ref[first : first + count, :] = turned[0:count]

    send_leaves(0)
    tile, sums = own_tile(pos_ref, mom_ref)
    msum = jnp.zeros((8, LANES), F32)
    for j in range(3):
        msum = jnp.where((sub == 7) & (lane == j), sums[j], msum)
    take_tile(tile, 0)
    send_cells(0, msum)
    finish_leaves(0, LEAVES)
    finish_cells(tile, 0, OWN)
    for b in range(SECTIONS):
        first = LEAVES + b * LEAF_SENDS
        leaf_copy(b).wait_recv()
        for s in range(LEAF_SENDS):
            pool_ref[first + s, 0:6, :] = recv_l[b, 6 * s : 6 * s + 6, :]
        if b + 1 < SECTIONS:
            send_leaves(b + 1)
        cell_copy(b).wait_recv()
        got = recv_c[b]
        low = jnp.where(lane < CELL_SENDS, pltpu.roll(got, CELL_SENDS, 1), 0.0)
        high = jnp.where(lane < CELL_SENDS, got, 0.0)
        tile = jnp.concatenate([high, low], axis=0)
        msum = msum + jnp.where(sub == 7, low, 0.0)
        if b + 1 < SECTIONS:
            take_tile(tile, b + 1)
            send_cells(b + 1, msum)
        finish_leaves(first, LEAF_SENDS)
        finish_cells(tile, OWN + b * CELL_SENDS, CELL_SENDS)
    scaled = msum * (-DEMAG / (N_DOM * LEAVES))
    unif_ref[...] = jnp.concatenate(
        [jnp.broadcast_to(scaled[7:8, j : j + 1], (1, LANES)) for j in range(3)]
        + [jnp.zeros((5, LANES), F32)],
        axis=0,
    )
    for b in range(SECTIONS):
        leaf_copy(b).wait_send()
        cell_copy(b).wait_send()


def exchange(positions, moments, fwd_leaves, fwd_counts, fwd_cells):
    vmem = pl.BlockSpec(memory_space=pltpu.VMEM)
    smem = pl.BlockSpec(memory_space=pltpu.SMEM)
    dma = pltpu.SemaphoreType.DMA((SECTIONS,))
    return pl.pallas_call(
        exchange_kernel,
        out_shape=(
            jax.ShapeDtypeStruct((LEAF_POOL, 8, LANES), F32),
            jax.ShapeDtypeStruct((CELL_POOL, LANES), F32),
            jax.ShapeDtypeStruct((8, LANES), F32),
        ),
        in_specs=[vmem, vmem, smem, smem, vmem],
        out_specs=(vmem, vmem, vmem),
        scratch_shapes=[
            pltpu.VMEM((48, (SECTIONS + 1) * LANES), BF16),
            pltpu.VMEM((16, LANES), jnp.int32),
            pltpu.VMEM((SECTIONS, 6 * LEAF_SENDS, LANES), F32),
            pltpu.VMEM((SECTIONS, 6 * LEAF_SENDS, LANES), F32),
            pltpu.VMEM((SECTIONS, 8, LANES), F32),
            pltpu.VMEM((SECTIONS, 8, LANES), F32),
            dma, dma, dma, dma,
        ],
        compiler_params=pltpu.CompilerParams(
            collective_id=0, has_side_effects=True, vmem_limit_bytes=40 * 1024 * 1024
        ),
        name="exchange",
    )(positions, moments, fwd_leaves, fwd_counts, fwd_cells)


def target_side(block, sub):
    cut = pieces(block)
    zero = jnp.zeros((8, LANES), F32)
    order = (0, 1, 2, 0, 1, 0)
    lead = (True, False, False, True, False, True)
    quad, along = [], []
    for p, flag in zip(order, lead):
        mark = 1.0 if flag else 0.0
        quad.append(jnp.where(sub < 3, -2.0 * cut[p], jnp.where(sub == 6, mark, 0.0)))
        turned = pltpu.roll(cut[p], 3, 0)
        along.append(
            jnp.where((sub >= 3) & (sub < 6), turned, jnp.where(sub == 7, -mark, 0.0))
        )
    quad.append(
        jnp.where(sub == 6, cut[0], jnp.where(sub == 7, pltpu.roll(cut[1], 1, 0), 0.0))
    )
    quad.append(jnp.where(sub == 6, cut[2], jnp.where(sub == 7, 1.0, 0.0)))
    along += [zero, zero]
    side = jnp.concatenate(
        [
            jnp.transpose(jnp.concatenate(quad, axis=0)),
            jnp.transpose(jnp.concatenate(along, axis=0)),
        ],
        axis=0,
    )
    return side.astype(BF16)


def near_item(side, block, sub):
    cut = pieces(block)
    source = jnp.concatenate(
        [cut[0], cut[0], cut[0], cut[1], cut[1], cut[2], jnp.ones((16, LANES), F32)], axis=0
    ).astype(BF16)
    both = jnp.dot(side, source, preferred_element_type=F32)
    inv = lax.rsqrt(both[0:LANES])
    inv2 = inv * inv
    inv3 = inv2 * inv
    coef = both[LANES:] * (inv3 * inv2)
    weights = jnp.concatenate([coef, inv3], axis=1)
    high = weights.astype(BF16)
    low = (weights - high.astype(F32)).astype(BF16)

    def sums(part, one):
        c_side = jnp.where(sub < 3, part, jnp.where(sub == 6, one, 0.0))
        w_side = jnp.where((sub >= 3) & (sub < 6), part, 0.0)
        return jnp.concatenate([c_side, w_side], axis=1)

    left = jnp.concatenate([sums(cut[0], 1.0), sums(cut[1], 0.0)], axis=0).astype(BF16)
    dims = (((1,), (1,)), ((), ()))
    got = lax.dot_general(left, high, dims, preferred_element_type=F32)
    got = got + lax.dot_general(left, low, dims, preferred_element_type=F32)
    return got[0:8] + got[8:16]


def far_item(x, rows):
    col = lambda p: jnp.broadcast_to(rows[:, p : p + 1], (8, LANES))
    sep = [x[d] - col(d) for d in range(3)]
    tot = [col(3 + d) for d in range(3)]
    xx, yy, zz, xy, xz, yz, trace = [col(6 + i) for i in range(7)]
    quad = sep[0] * sep[0] + sep[1] * sep[1] + sep[2] * sep[2] + 1.0
    inv = lax.rsqrt(quad)
    inv2 = inv * inv
    inv3 = inv2 * inv
    inv5 = 3.0 * (inv3 * inv2)
    inv7 = 2.5 * (inv5 * inv2)
    along = tot[0] * sep[0] + tot[1] * sep[1] + tot[2] * sep[2] - trace
    turn = [
        xx * sep[0] + xy * sep[1] + xz * sep[2],
        xy * sep[0] + yy * sep[1] + yz * sep[2],
        xz * sep[0] + yz * sep[1] + zz * sep[2],
    ]
    bend = sep[0] * turn[0] + sep[1] * turn[1] + sep[2] * turn[2]
    coef = along * inv5 + bend * inv7
    return [sep[d] * coef - tot[d] * inv3 - turn[d] * inv5 for d in range(3)]


def field_kernel(
    pool_ref, cells_ref, unif_ref, clist_ref, clen_ref, llist_ref, llen_ref,
    out_ref, sides, near, far,
):
    sub = iota((8, LANES), 0)

    def prepare(t, carry):
        sides[t] = target_side(pool_ref[t], sub)
        near[t] = jnp.zeros((8, LANES), F32)
        far[t] = jnp.zeros((3, 8, LANES), F32)
        return carry

    lax.fori_loop(0, LEAVES, prepare, 0)
    near[LEAVES] = jnp.zeros((8, LANES), F32)
    far[LEAVES] = jnp.zeros((3, 8, LANES), F32)

    def step(t, k, most):
        more = k + 1 < most
        return jnp.where(more, t, t + 1), jnp.where(more, k + 1, 0)

    def near_body(at):
        t, k = at
        todo = []
        for _ in range(NEAR_UNROLL):
            row = jnp.minimum(t, LEAVES - 1)
            todo.append((jnp.minimum(t, LEAVES), row, llist_ref[row, k]))
            t, k = step(t, k, llen_ref[row])
        parts = [near_item(sides[row], pool_ref[src], sub) for _, row, src in todo]
        for (slot, _, _), part in zip(todo, parts):
            near[slot] += part
        return t, k

    lax.while_loop(lambda at: at[0] < LEAVES, near_body, (jnp.int32(0), jnp.int32(0)))

    def far_body(at):
        t, k = at
        todo = []
        for _ in range(FAR_UNROLL):
            row = jnp.minimum(t, LEAVES - 1)
            most = clen_ref[row]
            todo.append((jnp.minimum(t, LEAVES), row, k, most))
            t, k = step(t, k, (most + 7) // 8)
        parts = []
        for _, row, group, most in todo:
            rows = jnp.concatenate(
                [cells_ref[pl.ds(clist_ref[row, 8 * group + i], 1), :] for i in range(8)], axis=0
            )
            rows = jnp.where(8 * group + sub < most, rows, 0.0)
            block = pool_ref[row]
            x = [jnp.broadcast_to(block[d : d + 1], (8, LANES)) for d in range(3)]
            parts.append(far_item(x, rows))
        for (slot, _, _, _), part in zip(todo, parts):
            for d in range(3):
                far[slot, d] += part[d]
        return t, k

    lax.while_loop(lambda at: at[0] < LEAVES, far_body, (jnp.int32(0), jnp.int32(0)))

    unif = unif_ref[0:3]

    def finish(t, carry):
        got = near[t]
        x = pool_ref[t][0:3]
        close = 3.0 * (x * got[6:7] - got[0:3]) - got[3:6]
        out_ref[t] = close + jnp.sum(far[t], axis=1) + unif
        return carry

    lax.fori_loop(0, LEAVES, finish, 0)


def field(pool, cells, unif, cell_list, cell_len, leaf_list, leaf_len):
    vmem = pl.BlockSpec(memory_space=pltpu.VMEM)
    smem = pl.BlockSpec(memory_space=pltpu.SMEM)
    return pl.pallas_call(
        field_kernel,
        out_shape=jax.ShapeDtypeStruct((LEAVES, 3, LANES), F32),
        in_specs=[vmem, vmem, vmem, smem, smem, smem, smem],
        out_specs=vmem,
        scratch_shapes=[
            pltpu.VMEM((LEAVES, 2 * LANES, 64), BF16),
            pltpu.VMEM((LEAVES + 1, 8, LANES), F32),
            pltpu.VMEM((LEAVES + 1, 3, 8, LANES), F32),
        ],
        compiler_params=pltpu.CompilerParams(vmem_limit_bytes=40 * 1024 * 1024),
        name="field",
    )(pool, cells, unif, cell_list, cell_len, leaf_list, leaf_len)


def per_device(
    positions, moments, fwd_cells, fwd_leaves, fwd_counts, cell_list, cell_len, leaf_list, leaf_len
):
    pool, cells, unif = exchange(positions, moments, fwd_leaves, fwd_counts, fwd_cells)
    return field(pool, cells, unif, cell_list, cell_len, leaf_list, leaf_len)


def solution(mesh):
    row = P("dom", None)
    cube = P("dom", None, None)
    return jax.shard_map(
        per_device,
        mesh=mesh,
        in_specs=(cube, cube, cube, cube, cube, row, P("dom"), row, P("dom")),
        out_specs=cube,
        check_vma=False,
    )
```

time: 465 us -> 126 us (0.27)
  the two profiles are of different devices: /device:TPU:6 before, /device:TPU:50 now
where the time goes in v1:
time: 126 us
  Pallas kernels  121 us (96%)
  local copies, waits for them, and re-layouts  4.42 us (4%)
    pallas_call x1, Pallas kernels, field(): pl.pallas_call(field_kernel, out_shape=jax.ShapeDtypeStruct((LEAVES, 3, L...  71.8 us
    pallas_call x1, Pallas kernels, exchange(): pl.pallas_call(exchange_kernel, out_shape=(jax.ShapeDtypeStruct((LEAF_POO...  49.6 us
    unnamed x22, local copies, waits for them, and re-layouts  3.78 us

profile of v1, /device:TPU:50, one launch (start us, length us, event | category | flops | bytes accessed | tf_op | source)
XLA Modules:
  0.0 125.8 jit_solution(3822772756613777111)
XLA Ops:
  0.0 0.0 copy-start.3
  0.0 1.0 copy.10.pos_ref
  1.0 0.0 copy-done.3
  1.0 0.0 copy-start.4
  1.0 0.1 copy.11.mom_ref
  1.1 0.6 copy-done.4
  1.7 0.0 copy-start.7
  1.7 0.7 copy-done.7
  2.4 0.0 copy-start.5
  2.4 0.1 copy.13.fn_ref
  2.5 0.6 copy-done.5
  3.1 0.0 copy-start.6
  3.1 49.6 %exchange.1 = (f32[244,8,128]{2,1,0:T(8,128)S(1)}, f32[648,128]{1,0:T(8,128)S(1)}, f32[8,128]{1,0:T(8,128)S(1)}) custom-call(f32[64,3,128]{2,1,0:T(4,128)S(1)} %copy.10.pos_ref, f32[64,3,128]{2,1,0:T(4,128)S(1)} %copy.11.mom_ref, s32[1,9,20]{2,1,0:T(8,128)S(1)} %copy.12.fl_ref, s32[1,9,2]{2,1,0:T(8,128)S(1)} %copy.13.fn_ref, s32[1,9,64]{2,1,0:T(8,128)S(1)} %copy.14.fc_ref), custom_call_target="tpu_custom_call" | custom-call | tf_op jit(solution)/shard_map/exchange/pallas_call | solution.py:211
  52.6 0.0 copy-start
  52.7 0.0 copy-done.6
  52.7 0.0 copy-start.1
  52.7 0.0 copy-start.2
  52.7 0.1 copy.15.llist_ref
  52.8 0.6 copy-done
  53.4 0.0 copy-done.1
  53.4 0.0 copy-done.2
  53.4 71.8 %field.1 = f32[64,3,128]{2,1,0:T(4,128)S(1)} custom-call(f32[244,8,128]{2,1,0:T(8,128)S(1)} %get-tuple-element.8.pool_ref, f32[648,128]{1,0:T(8,128)S(1)} %get-tuple-element.9.cells_ref, f32[8,128]{1,0:T(8,128)S(1)} %get-tuple-element.10.unif_ref, s32[64,64]{1,0:T(8,128)S(1)} %copy-done, s32[64]{0:T(128)S(1)} %copy-done.1, s32[64,8]{1,0:T(8,128)S(1)} %copy.15.llist_ref, ...), custom_call_target="tpu_custom_call" | custom-call | tf_op jit(solution)/shard_map/field/pallas_call | solution.py:385
  125.2 0.6 copy.16
  (2 shorter events, 0.0 us)
Async XLA Ops:
  0.0 1.0 copy-start.3
  1.0 0.7 copy-start.4
  1.7 0.7 copy-start.7
  2.4 0.7 copy-start.5
  3.1 49.6 %copy-start.6 = (s32[64,8]{0,1:T(8,128)S(1)}, s32[64,8]{0,1:T(8,128)}, u32[]{:S(2)}) copy-start(s32[64,8]{0,1:T(8,128)} %param.16) | copy-start | bytes 6148
  52.6 0.8 copy-start
  52.7 0.7 copy-start.1
  52.7 0.7 copy-start.2

commit v2 on v1

--- a/solution.py
+++ b/solution.py
@@ -21,7 +21,7 @@
 LANES = 128
 N_DOM = 512
 NEAR_UNROLL = 4
-FAR_UNROLL = 4
+FAR_UNROLL = 8
 
 
 def iota(shape, dim):
@@ -235,7 +235,7 @@
 
 def target_side(block, sub):
     cut = pieces(block)
-    zero = jnp.zeros((8, LANES), F32)
+    zero = jnp.zeros((16, LANES), F32)
     order = (0, 1, 2, 0, 1, 0)
     lead = (True, False, False, True, False, True)
     quad, along = [], []
@@ -250,41 +250,48 @@
         jnp.where(sub == 6, cut[0], jnp.where(sub == 7, pltpu.roll(cut[1], 1, 0), 0.0))
     )
     quad.append(jnp.where(sub == 6, cut[2], jnp.where(sub == 7, 1.0, 0.0)))
-    along += [zero, zero]
-    side = jnp.concatenate(
-        [
-            jnp.transpose(jnp.concatenate(quad, axis=0)),
-            jnp.transpose(jnp.concatenate(along, axis=0)),
-        ],
-        axis=0,
-    )
-    return side.astype(BF16)
-
-
-def near_item(side, block, sub):
+    along.append(zero)
+    return jnp.concatenate(
+        [jnp.concatenate(quad, axis=0), jnp.concatenate(along, axis=0)], axis=1
+    ).astype(BF16)
+
+
+def near_product(side, block):
     cut = pieces(block)
     source = jnp.concatenate(
         [cut[0], cut[0], cut[0], cut[1], cut[1], cut[2], jnp.ones((16, LANES), F32)], axis=0
     ).astype(BF16)
-    both = jnp.dot(side, source, preferred_element_type=F32)
-    inv = lax.rsqrt(both[0:LANES])
-    inv2 = inv * inv
-    inv3 = inv2 * inv
-    coef = both[LANES:] * (inv3 * inv2)
-    weights = jnp.concatenate([coef, inv3], axis=1)
-    high = weights.astype(BF16)
-    low = (weights - high.astype(F32)).astype(BF16)
+    return lax.dot_general(
+        source, side, (((0,), (0,)), ((), ())), preferred_element_type=F32
+    )
+
+
+def near_sums(both, block, sub):
+    parts = [[], [], [], []]
+    for c in range(LANES // 16):
+        quad = both[16 * c : 16 * c + 16, 0:LANES]
+        along = both[16 * c : 16 * c + 16, LANES:]
+        inv = lax.rsqrt(quad)
+        inv2 = inv * inv
+        inv3 = inv2 * inv
+        coef = along * (inv3 * inv2)
+        for i, weight in enumerate((coef, inv3)):
+            high = weight.astype(BF16)
+            parts[i].append(high)
+            parts[2 + i].append((weight - high.astype(F32)).astype(BF16))
+    high = jnp.concatenate(parts[0] + parts[1], axis=0)
+    low = jnp.concatenate(parts[2] + parts[3], axis=0)
 
     def sums(part, one):
         c_side = jnp.where(sub < 3, part, jnp.where(sub == 6, one, 0.0))
         w_side = jnp.where((sub >= 3) & (sub < 6), part, 0.0)
         return jnp.concatenate([c_side, w_side], axis=1)
 
+    cut = pieces(block)
     left = jnp.concatenate([sums(cut[0], 1.0), sums(cut[1], 0.0)], axis=0).astype(BF16)
-    dims = (((1,), (1,)), ((), ()))
-    got = lax.dot_general(left, high, dims, preferred_element_type=F32)
-    got = got + lax.dot_general(left, low, dims, preferred_element_type=F32)
-    return got[0:8] + got[8:16]
+    got = jnp.dot(left, high, preferred_element_type=F32)
+    more = jnp.dot(left, low, preferred_element_type=F32)
+    return (got[0:8] + got[8:16]) + more[0:8]
 
 
 def far_item(x, rows):
@@ -311,7 +318,7 @@
 
 def field_kernel(
     pool_ref, cells_ref, unif_ref, clist_ref, clen_ref, llist_ref, llen_ref,
-    out_ref, sides, near, far,
+    out_ref, sides, near, far, buf_a, buf_b,
 ):
     sub = iota((8, LANES), 0)
 
@@ -329,19 +336,40 @@
         more = k + 1 < most
         return jnp.where(more, t, t + 1), jnp.where(more, k + 1, 0)
 
-    def near_body(at):
+    def near_items(at):
         t, k = at
         todo = []
         for _ in range(NEAR_UNROLL):
             row = jnp.minimum(t, LEAVES - 1)
-            todo.append((jnp.minimum(t, LEAVES), row, llist_ref[row, k]))
+            todo += [jnp.minimum(t, LEAVES), llist_ref[row, k]]
             t, k = step(t, k, llen_ref[row])
-        parts = [near_item(sides[row], pool_ref[src], sub) for _, row, src in todo]
-        for (slot, _, _), part in zip(todo, parts):
-            near[slot] += part
-        return t, k
-
-    lax.while_loop(lambda at: at[0] < LEAVES, near_body, (jnp.int32(0), jnp.int32(0)))
+        return (t, k), tuple(todo)
+
+    def near_first(todo, buf):
+        for i in range(NEAR_UNROLL):
+            row = jnp.minimum(todo[2 * i], LEAVES - 1)
+            buf[i] = near_product(sides[row], pool_ref[todo[2 * i + 1]])
+
+    def near_last(todo, buf):
+        parts = []
+        for i in range(NEAR_UNROLL):
+            parts.append(near_sums(buf.at[i], pool_ref[todo[2 * i + 1]], sub))
+        for i in range(NEAR_UNROLL):
+            near[todo[2 * i]] += parts[i]
+
+    def near_body(carry):
+        at, now = carry
+        at, then = near_items(at)
+        near_first(then, buf_b)
+        near_last(now, buf_a)
+        at, now = near_items(at)
+        near_first(now, buf_a)
+        near_last(then, buf_b)
+        return at, now
+
+    at, now = near_items((jnp.int32(0), jnp.int32(0)))
+    near_first(now, buf_a)
+    lax.while_loop(lambda carry: carry[1][0] < LEAVES, near_body, (at, now))
 
     def far_body(at):
         t, k = at
@@ -388,9 +416,11 @@
         in_specs=[vmem, vmem, vmem, smem, smem, smem, smem],
         out_specs=vmem,
         scratch_shapes=[
-            pltpu.VMEM((LEAVES, 2 * LANES, 64), BF16),
+            pltpu.VMEM((LEAVES, 64, 2 * LANES), BF16),
             pltpu.VMEM((LEAVES + 1, 8, LANES), F32),
             pltpu.VMEM((LEAVES + 1, 3, 8, LANES), F32),
+            pltpu.VMEM((NEAR_UNROLL, LANES, 2 * LANES), F32),
+            pltpu.VMEM((NEAR_UNROLL, LANES, 2 * LANES), F32),
         ],
         compiler_params=pltpu.CompilerParams(vmem_limit_bytes=40 * 1024 * 1024),
         name="field",

time: 126 us -> 89.1 us (0.71)
  the two profiles are of different devices: /device:TPU:50 before, /device:TPU:60 now
where the time goes in v2:
time: 89.1 us; the launch traced here: 88.8 us
  Pallas kernels  84.3 us (95%)
  local copies, waits for them, and re-layouts  4.42 us (5%)
    pallas_call x1, Pallas kernels, exchange(): pl.pallas_call(exchange_kernel, out_shape=(jax.ShapeDtypeStruct((LEAF_POO...  49.4 us
    pallas_call x1, Pallas kernels, field(): pl.pallas_call(field_kernel, out_shape=jax.ShapeDtypeStruct((LEAVES, 3, L...  34.9 us
    unnamed x22, local copies, waits for them, and re-layouts  3.78 us

profile of v2, /device:TPU:60, one launch (start us, length us, event | category | flops | bytes accessed | tf_op | source)
XLA Modules:
  0.0 88.8 jit_solution(17625555176593423104)
XLA Ops:
  0.0 0.0 copy-start.3
  0.0 1.0 %copy.10.pos_ref = f32[64,3,128]{2,1,0:T(4,128)S(1)} copy(f32[64,3,128]{2,0,1:T(8,128)} %param.9) | data formatting | bytes 196608 | tf_op args[0]
  1.0 0.0 copy-done.3
  1.0 0.0 copy-start.4
  1.0 0.1 copy.11.mom_ref
  1.1 0.6 copy-done.4
  1.7 0.0 copy-start.7
  1.7 0.7 copy-done.7
  2.4 0.0 copy-start.5
  2.4 0.1 copy.13.fn_ref
  2.5 0.6 copy-done.5
  3.1 0.0 copy-start.6
  3.1 49.4 %exchange.1 = (f32[244,8,128]{2,1,0:T(8,128)S(1)}, f32[648,128]{1,0:T(8,128)S(1)}, f32[8,128]{1,0:T(8,128)S(1)}) custom-call(f32[64,3,128]{2,1,0:T(4,128)S(1)} %copy.10.pos_ref, f32[64,3,128]{2,1,0:T(4,128)S(1)} %copy.11.mom_ref, s32[1,9,20]{2,1,0:T(8,128)S(1)} %copy.12.fl_ref, s32[1,9,2]{2,1,0:T(8,128)S(1)} %copy.13.fn_ref, s32[1,9,64]{2,1,0:T(8,128)S(1)} %copy.14.fc_ref), custom_call_target="tpu_custom_call" | custom-call | tf_op jit(solution)/shard_map/exchange/pallas_call | solution.py:211
  52.5 0.0 copy-start
  52.5 0.0 copy-done.6
  52.5 0.0 copy-start.1
  52.5 0.0 copy-start.2
  52.5 0.1 copy.15.llist_ref
  52.6 0.6 copy-done
  53.2 0.0 copy-done.1
  53.2 0.0 copy-done.2
  53.2 34.9 %field.1 = f32[64,3,128]{2,1,0:T(4,128)S(1)} custom-call(f32[244,8,128]{2,1,0:T(8,128)S(1)} %get-tuple-element.8.pool_ref, f32[648,128]{1,0:T(8,128)S(1)} %get-tuple-element.9.cells_ref, f32[8,128]{1,0:T(8,128)S(1)} %get-tuple-element.10.unif_ref, s32[64,64]{1,0:T(8,128)S(1)} %copy-done, s32[64]{0:T(128)S(1)} %copy-done.1, s32[64,8]{1,0:T(8,128)S(1)} %copy.15.llist_ref, ...), custom_call_target="tpu_custom_call" | custom-call | tf_op jit(solution)/shard_map/field/pallas_call | solution.py:413
  88.1 0.6 copy.16
  (2 shorter events, 0.0 us)
Async XLA Ops:
  0.0 1.0 %copy-start.3 = (f32[64,3,128]{2,0,1:T(8,128)S(1)}, f32[64,3,128]{2,0,1:T(8,128)}, u32[]{:S(2)}) copy-start(f32[64,3,128]{2,0,1:T(8,128)} %param.10) | copy-start | bytes 294916
  1.0 0.7 copy-start.4
  1.7 0.7 copy-start.7
  2.4 0.7 copy-start.5
  3.1 49.4 %copy-start.6 = (s32[64,8]{0,1:T(8,128)S(1)}, s32[64,8]{0,1:T(8,128)}, u32[]{:S(2)}) copy-start(s32[64,8]{0,1:T(8,128)} %param.16) | copy-start | bytes 6148
  52.5 0.8 copy-start
  52.5 0.7 copy-start.1
  52.5 0.7 copy-start.2

commit v3 on v1

v3 whole, which is shorter than its diff:
```python
import functools

import jax
import jax.numpy as jnp
from jax import lax
from jax.experimental import pallas as pl
from jax.experimental.pallas import tpu as pltpu
from jax.sharding import PartitionSpec as P

F32 = jnp.float32
BF16 = jnp.bfloat16
DEMAG = 4.1887902047863905
LEAVES = 64
PARENTS = 8
OWN = LEAVES + PARENTS
SECTIONS = 9
CELL_SENDS = 64
LEAF_SENDS = 20
LEAF_POOL = LEAVES + SECTIONS * LEAF_SENDS
WIDE = 128 + SECTIONS * CELL_SENDS
LANES = 128
N_DOM = 512
NEAR_UNROLL = 4
FAR_UNROLL = 2


def iota(shape, dim):
    return lax.broadcasted_iota(jnp.int32, shape, dim)


def pieces(x):
    first = x.astype(BF16).astype(F32)
    rest = x - first
    second = rest.astype(BF16).astype(F32)
    return first, second, rest - second


def cell_features(tile):
    row = lambda i: tile[i : i + 1]
    sec = lambda k, j: row(6 + 3 * k + j)
    c = [row(d) for d in range(3)]
    tot = [row(3 + d) for d in range(3)]
    xx, yy, zz = [2.0 * sec(d, d) for d in range(3)]
    xy, xz, yz = sec(0, 1) + sec(1, 0), sec(0, 2) + sec(2, 0), sec(1, 2) + sec(2, 1)
    turn = [
        xx * c[0] + xy * c[1] + xz * c[2],
        xy * c[0] + yy * c[1] + yz * c[2],
        xz * c[0] + yz * c[1] + zz * c[2],
    ]
    main = jnp.concatenate(
        [tile[0:6], xx, yy, zz, xy, xz, yz] + turn + [jnp.ones((1, LANES), F32)], axis=0
    )
    rest = jnp.concatenate(
        [
            c[0] * c[0] + c[1] * c[1] + c[2] * c[2] + 1.0,
            -(tot[0] * c[0] + tot[1] * c[1] + tot[2] * c[2])
            - (sec(0, 0) + sec(1, 1) + sec(2, 2)),
            c[0] * turn[0] + c[1] * turn[1] + c[2] * turn[2],
        ],
        axis=0,
    )
    blocks = list(pieces(main)) + list(pieces(rest)) + [jnp.zeros((7, LANES), F32)]
    return jnp.concatenate(blocks, axis=0).astype(BF16)


def far_side(block):
    x = [block[d : d + 1] for d in range(3)]
    none = lambda n: jnp.zeros((n, LANES), F32)
    x3 = block[0:3]
    quad = jnp.concatenate([-2.0 * x3, none(12), block[6:7]], axis=0)
    along = jnp.concatenate([none(3), x3, none(10)], axis=0)
    bend = jnp.concatenate(
        [
            none(6), x[0] * x[0], x[1] * x[1], x[2] * x[2],
            2.0 * (x[0] * x[1]), 2.0 * (x[0] * x[2]), 2.0 * (x[1] * x[2]),
            -2.0 * x3, none(1),
        ],
        axis=0,
    )
    sub = iota((16, LANES), 0)
    cols = []
    for i, part in enumerate((quad, along, bend)):
        p0, p1, p2 = pieces(part)
        ones = jnp.where((sub < 9) & (lax.rem(sub, 3) == i), 1.0, 0.0)
        cols.append(jnp.concatenate([p0, p1, p2, p0, p1, p0, ones], axis=0).astype(BF16))
    return jnp.concatenate(cols, axis=1)


def far_product(side, picked):
    a0, a1, a2, rest = picked[0:16], picked[16:32], picked[32:48], picked[48:64]
    stack = jnp.concatenate([a0, a0, a0, a1, a1, a2, rest], axis=0).astype(BF16)
    return lax.dot_general(stack, side, (((0,), (0,)), ((), ())), preferred_element_type=F32)


def far_sums(both, picked, block):
    quad = jnp.maximum(both[:, 0:LANES], 1.0)
    inv = lax.rsqrt(quad)
    inv2 = inv * inv
    inv3 = inv2 * inv
    inv5 = 3.0 * (inv3 * inv2)
    inv7 = 2.5 * (inv5 * inv2)
    coef = both[:, LANES : 2 * LANES] * inv5 + both[:, 2 * LANES :] * inv7
    sub = iota((16, 64), 0)

    def lefts(part, one):
        first = jnp.where(sub < 3, part, jnp.where(sub == 3, one, 0.0))
        second = jnp.where(sub < 3, pltpu.roll(part, 13, 0), 0.0)
        third = jnp.where(
            sub < 3,
            -pltpu.roll(part, 4, 0),
            jnp.where((sub >= 4) & (sub < 10), pltpu.roll(part, 14, 0), 0.0),
        )
        return first, second, third

    total = None
    for weight, high_l, low_l in zip(
        (coef, inv3, inv5), lefts(picked[0:16], 1.0), lefts(picked[16:32], 0.0)
    ):
        high = weight.astype(BF16)
        low = (weight - high.astype(F32)).astype(BF16)
        left = jnp.concatenate([high_l, low_l], axis=0).astype(BF16)
        part = jnp.dot(
            left, jnp.concatenate([high, low], axis=1), preferred_element_type=F32
        )
        total = part if total is None else total + part
    got = (total[0:16, 0:LANES] + total[16:32, 0:LANES]) + total[0:16, LANES:]
    x = [block[d : d + 1] for d in range(3)]
    q = [got[4 + i : 5 + i] for i in range(6)]
    turn = [
        q[0] * x[0] + q[3] * x[1] + q[4] * x[2],
        q[3] * x[0] + q[1] * x[1] + q[5] * x[2],
        q[4] * x[0] + q[5] * x[1] + q[2] * x[2],
    ]
    return [x[d] * got[3:4] - got[d : d + 1] - turn[d] for d in range(3)]


def own_tile(pos_ref, mom_ref):
    pos = [pos_ref[:, k, :] for k in range(3)]
    mom = [mom_ref[:, k, :] for k in range(3)]
    cen = [jnp.sum(p, axis=1, keepdims=True) * (1.0 / LANES) for p in pos]
    tot = [jnp.sum(m, axis=1, keepdims=True) for m in mom]
    off = [pos[k] - cen[k] for k in range(3)]
    sec = [
        [jnp.sum(off[k] * mom[j], axis=1, keepdims=True) for j in range(3)] for k in range(3)
    ]
    full = lambda x: jnp.broadcast_to(x, (LEAVES, LANES)).reshape(PARENTS, 8, LANES)
    fcen = [full(c) for c in cen]
    ftot = [full(c) for c in tot]
    fsec = [[full(sec[k][j]) for j in range(3)] for k in range(3)]
    pcen = [jnp.sum(c, axis=1, keepdims=True) * 0.125 for c in fcen]
    ptot = [jnp.sum(c, axis=1) for c in ftot]
    psec = [
        [jnp.sum(fsec[k][j] + (fcen[k] - pcen[k]) * ftot[j], axis=1) for j in range(3)]
        for k in range(3)
    ]
    leaf = fcen + ftot + [fsec[k][j] for k in range(3) for j in range(3)]
    up = [c[:, 0, :] for c in pcen] + ptot + [psec[k][j] for k in range(3) for j in range(3)]
    lane = iota((LEAVES, LANES), 1)
    lane_p = iota((PARENTS, LANES), 1)
    rows = jnp.zeros((LEAVES, LANES), F32)
    rows_p = jnp.zeros((PARENTS, LANES), F32)
    for i in range(15):
        rows = jnp.where(lane == i, leaf[i].reshape(LEAVES, LANES), rows)
        rows_p = jnp.where(lane_p == i, up[i], rows_p)
    every = jnp.concatenate([rows, rows_p, jnp.zeros((LANES - OWN, LANES), F32)], axis=0)
    sums = [jnp.sum(p, axis=0, keepdims=True) for p in ptot]
    return jnp.transpose(every)[0:16], sums


def target_side(block, sub):
    cut = pieces(block)
    zero = jnp.zeros((16, LANES), F32)
    order = (0, 1, 2, 0, 1, 0)
    lead = (True, False, False, True, False, True)
    quad, along = [], []
    for p, flag in zip(order, lead):
        mark = 1.0 if flag else 0.0
        quad.append(jnp.where(sub < 3, -2.0 * cut[p], jnp.where(sub == 6, mark, 0.0)))
        turned = pltpu.roll(cut[p], 3, 0)
        along.append(
            jnp.where((sub >= 3) & (sub < 6), turned, jnp.where(sub == 7, -mark, 0.0))
        )
    quad.append(
        jnp.where(sub == 6, cut[0], jnp.where(sub == 7, pltpu.roll(cut[1], 1, 0), 0.0))
    )
    quad.append(jnp.where(sub == 6, cut[2], jnp.where(sub == 7, 1.0, 0.0)))
    along.append(zero)
    return jnp.concatenate(
        [jnp.concatenate(quad, axis=0), jnp.concatenate(along, axis=0)], axis=1
    ).astype(BF16)


def near_product(side, block):
    cut = pieces(block)
    source = jnp.concatenate(
        [cut[0], cut[0], cut[0], cut[1], cut[1], cut[2], jnp.ones((16, LANES), F32)], axis=0
    ).astype(BF16)
    return lax.dot_general(
        source, side, (((0,), (0,)), ((), ())), preferred_element_type=F32
    )


def near_sums(both, block, sub):
    parts = [[], [], [], []]
    for c in range(LANES // 16):
        quad = both[16 * c : 16 * c + 16, 0:LANES]
        along = both[16 * c : 16 * c + 16, LANES:]
        inv = lax.rsqrt(quad)
        inv2 = inv * inv
        inv3 = inv2 * inv
        coef = along * (inv3 * inv2)
        for i, weight in enumerate((coef, inv3)):
            high = weight.astype(BF16)
            parts[i].append(high)
            parts[2 + i].append((weight - high.astype(F32)).astype(BF16))
    high = jnp.concatenate(parts[0] + parts[1], axis=0)
    low = jnp.concatenate(parts[2] + parts[3], axis=0)

    def sums(part, one):
        c_side = jnp.where(sub < 3, part, jnp.where(sub == 6, one, 0.0))
        w_side = jnp.where((sub >= 3) & (sub < 6), part, 0.0)
        return jnp.concatenate([c_side, w_side], axis=1)

    cut = pieces(block)
    left = jnp.concatenate([sums(cut[0], 1.0), sums(cut[1], 0.0)], axis=0).astype(BF16)
    got = jnp.dot(left, high, preferred_element_type=F32)
    more = jnp.dot(left, low, preferred_element_type=F32)
    return (got[0:8] + got[8:16]) + more[0:8]


def near_pass(count, first, last, buf_a, buf_b):
    first(0, buf_a)

    def body(i, carry):
        g = 2 * i
        first(g + 1, buf_b)
        last(g, buf_a)
        first(jnp.minimum(g + 2, count - 1), buf_a)
        last(g + 1, buf_b)
        return carry

    lax.fori_loop(0, count // 2, body, 0)


def exchange_kernel(
    pos_ref, mom_ref, fl_ref, fn_ref, fc_ref, llist_ref, llen_ref, clist_ref, clen_ref,
    pool_ref, sides, near, far_ref,
    split, feats, index, cindex, gath, pick, fsides, buf_a, buf_b, far_a, far_b,
    send_l, recv_l, send_c, recv_c, sl_sem, rl_sem, sc_sem, rc_sem,
):
    me = lax.axis_index("dom")
    partners = []
    for b in range(SECTIONS):
        stride = 1 << b
        partners.append(me + (1 - 2 * lax.rem(me // stride, 2)) * stride)
    barrier = pltpu.get_barrier_semaphore()
    for other in partners:
        pl.semaphore_signal(
            barrier, inc=1, device_id=(other,), device_id_type=pl.DeviceIdType.MESH
        )
    pool_ref[0:LEAVES, 0:3, :] = pos_ref[...]
    pool_ref[0:LEAVES, 3:6, :] = mom_ref[...]

    lane = iota((8, LANES), 1)
    sub = iota((8, LANES), 0)
    index[...] = jnp.full((16, LANES), -1, jnp.int32)
    index[0:SECTIONS, 0:CELL_SENDS] = fc_ref[0]
    raw = index[...]
    index[...] = jnp.where(raw < OWN, raw, raw + (LANES - OWN))
    for half in range(2):
        rows = clist_ref[half * 32 : half * 32 + 32, :]
        cindex[:, half * 64 : half * 64 + 64] = jnp.where(
            rows < OWN, rows, rows + (LANES - OWN)
        )
    pl.semaphore_wait(barrier, SECTIONS)

    def leaf_copy(b):
        return pltpu.make_async_remote_copy(
            src_ref=send_l.at[b], dst_ref=recv_l.at[b],
            send_sem=sl_sem.at[b], recv_sem=rl_sem.at[b],
            device_id=(partners[b],), device_id_type=pl.DeviceIdType.MESH,
        )

    def cell_copy(b):
        return pltpu.make_async_remote_copy(
            src_ref=send_c.at[b], dst_ref=recv_c.at[b],
            send_sem=sc_sem.at[b], recv_sem=rc_sem.at[b],
            device_id=(partners[b],), device_id_type=pl.DeviceIdType.MESH,
        )

    def send_leaves(b):
        live = fn_ref[0, b, 1]
        for s in range(LEAF_SENDS):
            block = pool_ref[fl_ref[0, b, s]][0:6]
            send_l[b, 6 * s : 6 * s + 6, :] = jnp.where(s < live, block, 0.0)
        leaf_copy(b).start()

    def take_tile(tile, at, ref, rows):
        if at % 2:
            kept = ref[:, at // 2 * LANES : at // 2 * LANES + LANES]
            turned = pltpu.roll(rows.astype(F32), CELL_SENDS, 1).astype(BF16)
            wide = iota(rows.shape, 1)
            rows = jnp.where(wide < CELL_SENDS, kept.astype(F32), turned.astype(F32)).astype(BF16)
        ref[:, at // 2 * LANES : at // 2 * LANES + LANES] = rows

    def take_split(tile, at):
        take_tile(tile, at, split, jnp.concatenate(pieces(tile), axis=0).astype(BF16))

    def take_features(tile, at):
        take_tile(tile, at, feats, cell_features(tile))

    def send_cells(b, msum):
        depth = LANES * ((b + 3) // 2)
        wanted = jnp.where(lane[0:1] < fn_ref[0, b, 0], index[b : b + 1, :], -1)
        hot = jnp.where(iota((depth, LANES), 0) == wanted, 1.0, 0.0).astype(BF16)
        got = jnp.dot(split[:, 0:depth], hot, preferred_element_type=F32)
        got = (got[0:16] + got[16:32]) + got[32:48]
        low = jnp.where(sub == 7, msum, got[8:16])
        send_c[b] = jnp.where(lane < CELL_SENDS, got[0:8], pltpu.roll(low, CELL_SENDS, 1))
        cell_copy(b).start()

    def finish_leaves(first, count):
        part = [pool_ref[first : first + count, i, :] for i in range(6)]
        pool_ref[first : first + count, 6, :] = (
            part[0] * part[0] + part[1] * part[1] + part[2] * part[2]
        )
        pool_ref[first : first + count, 7, :] = (
            part[0] * part[3] + part[1] * part[4] + part[2] * part[5]
        )

    def prepare(t, carry):
        block = pool_ref[t]
        sides[t] = target_side(block, sub)
        fsides[t] = far_side(block)
        return carry

    def near_source(t, k):
        if k == 0:
            return pool_ref[t]
        return jnp.where(llen_ref[t] > 1, pool_ref[llist_ref[t, 1]], 0.0)

    def near_steps(t0, count):
        def first(g, buf):
            for i in range(4):
                t = t0 + 2 * g + i // 2
                buf[i] = near_product(sides[t], near_source(t, i % 2))

        def last(g, buf):
            for i in range(2):
                t = t0 + 2 * g + i
                near[t] = near_sums(buf.at[2 * i], near_source(t, 0), sub) + near_sums(
                    buf.at[2 * i + 1], near_source(t, 1), sub
                )

        near_pass(count // 2, first, last, buf_a, buf_b)

    def wanted_cells(i):
        row = cindex[pl.ds(i, 1), :]
        k = jnp.where(lane[0:1] < 64, lane[0:1], lane[0:1] - 64)
        most = jnp.where(lane[0:1] < 64, clen_ref[i], clen_ref[i + 32])
        return jnp.where(k < most, row, -1)

    old = LANES + (SECTIONS - 1) * CELL_SENDS

    def gather_old(g, carry):
        for j in range(2):
            i = 2 * g + j
            hot = jnp.where(iota((old, LANES), 0) == wanted_cells(i), 1.0, 0.0).astype(BF16)
            gath[i] = jnp.dot(feats[:, 0:old], hot, preferred_element_type=F32)
        return carry

    def far_first(g, buf):
        for j in range(FAR_UNROLL):
            i = FAR_UNROLL * g + j
            hot = jnp.where(
                iota((LANES, LANES), 0) + old == wanted_cells(i), 1.0, 0.0
            ).astype(BF16)
            picked = gath[i] + jnp.dot(
                feats[:, old : old + LANES], hot, preferred_element_type=F32
            )
            pick[i] = picked
            buf[2 * j] = far_product(fsides[i], picked[:, 0:64])
            buf[2 * j + 1] = far_product(fsides[i + 32], pltpu.roll(picked, 64, 1)[:, 0:64])

    def far_last(g, buf, unif):
        for j in range(FAR_UNROLL):
            i = FAR_UNROLL * g + j
            for half in range(2):
                picked = pick[i, 0:32]
                if half:
                    picked = pltpu.roll(picked, 64, 1)
                t = i + 32 * half
                parts = far_sums(buf[2 * j + half], picked[:, 0:64], pool_ref[t])
                for d in range(3):
                    far_ref[t, d : d + 1, :] = parts[d] + unif[d]

    def beside(b):
        if b == 0:
            finish_leaves(0, LEAVES)
            lax.fori_loop(0, LEAVES, prepare, 0)
        elif b < 5:
            near_steps(16 * (b - 1), 16)
        elif b == SECTIONS - 1:
            lax.fori_loop(0, 16, gather_old, 0)

    send_leaves(0)
    tile, sums = own_tile(pos_ref, mom_ref)
    msum = jnp.zeros((8, LANES), F32)
    for j in range(3):
        msum = jnp.where((sub == 7) & (lane == j), sums[j], msum)
    take_split(tile, 0)
    send_cells(0, msum)
    take_features(tile, 0)
    beside(0)
    for b in range(SECTIONS):
        first = LEAVES + b * LEAF_SENDS
        leaf_copy(b).wait_recv()
        for s in range(LEAF_SENDS):
            pool_ref[first + s, 0:6, :] = recv_l[b, 6 * s : 6 * s + 6, :]
        if b + 1 < SECTIONS:
            send_leaves(b + 1)
        cell_copy(b).wait_recv()
        got = recv_c[b]
        low = jnp.where(lane < CELL_SENDS, pltpu.roll(got, CELL_SENDS, 1), 0.0)
        high = jnp.where(lane < CELL_SENDS, got, 0.0)
        tile = jnp.concatenate([high, low], axis=0)
        msum = msum + jnp.where(sub == 7, low, 0.0)
        if b + 1 < SECTIONS:
            take_split(tile, b + 2)
            send_cells(b + 1, msum)
        take_features(tile, b + 2)
        finish_leaves(first, LEAF_SENDS)
        if b + 1 < SECTIONS:
            beside(b + 1)
    scaled = msum * (-DEMAG / (N_DOM * LEAVES))
    unif = [jnp.broadcast_to(scaled[7:8, j : j + 1], (1, LANES)) for j in range(3)]
    near_pass(
        32 // FAR_UNROLL, far_first, lambda g, buf: far_last(g, buf, unif), far_a, far_b
    )
    for b in range(SECTIONS):
        leaf_copy(b).wait_send()
        cell_copy(b).wait_send()


def exchange(
    positions, moments, fwd_leaves, fwd_counts, fwd_cells, leaf_list, leaf_len, cell_list, cell_len
):
    vmem = pl.BlockSpec(memory_space=pltpu.VMEM)
    smem = pl.BlockSpec(memory_space=pltpu.SMEM)
    dma = pltpu.SemaphoreType.DMA((SECTIONS,))
    return pl.pallas_call(
        exchange_kernel,
        out_shape=(
            jax.ShapeDtypeStruct((LEAF_POOL, 8, LANES), F32),
            jax.ShapeDtypeStruct((LEAVES, 64, 2 * LANES), BF16),
            jax.ShapeDtypeStruct((LEAVES, 8, LANES), F32),
            jax.ShapeDtypeStruct((LEAVES, 3, LANES), F32),
        ),
        in_specs=[vmem, vmem, smem, smem, vmem, smem, smem, vmem, smem],
        out_specs=(vmem, vmem, vmem, vmem),
        scratch_shapes=[
            pltpu.VMEM((48, WIDE + 64), BF16),
            pltpu.VMEM((64, WIDE + 64), BF16),
            pltpu.VMEM((16, LANES), jnp.int32),
            pltpu.VMEM((32, LANES), jnp.int32),
            pltpu.VMEM((32, 64, LANES), F32),
            pltpu.VMEM((32, 64, LANES), F32),
            pltpu.VMEM((LEAVES, 112, 3 * LANES), BF16),
            pltpu.VMEM((4, LANES, 2 * LANES), F32),
            pltpu.VMEM((4, LANES, 2 * LANES), F32),
            pltpu.VMEM((2 * FAR_UNROLL, 64, 3 * LANES), F32),
            pltpu.VMEM((2 * FAR_UNROLL, 64, 3 * LANES), F32),
            pltpu.VMEM((SECTIONS, 6 * LEAF_SENDS, LANES), F32),
            pltpu.VMEM((SECTIONS, 6 * LEAF_SENDS, LANES), F32),
            pltpu.VMEM((SECTIONS, 8, LANES), F32),
            pltpu.VMEM((SECTIONS, 8, LANES), F32),
            dma, dma, dma, dma,
        ],
        compiler_params=pltpu.CompilerParams(
            collective_id=0, has_side_effects=True, vmem_limit_bytes=40 * 1024 * 1024
        ),
        name="exchange",
    )(
        positions, moments, fwd_leaves, fwd_counts, fwd_cells,
        leaf_list, leaf_len, cell_list, cell_len,
    )


def field_kernel(
    pool_ref, sides, near0, far_ref, llist_ref, llen_ref, out_ref, near, todo_ref, buf_a, buf_b
):
    sub = iota((8, LANES), 0)

    def collect(t, count):
        todo_ref[count] = t
        return jnp.where(llen_ref[t] > 2, count + 1, count)

    busy = lax.fori_loop(0, LEAVES, collect, 0)
    near[0:LEAVES] = near0[...]
    near[LEAVES] = jnp.zeros((8, LANES), F32)

    def near_items(at):
        n, k = at
        todo = []
        for _ in range(NEAR_UNROLL):
            t = todo_ref[jnp.minimum(n, LEAVES - 1)]
            t = jnp.where(n < busy, t, 0)
            todo += [jnp.where(n < busy, t, LEAVES), t, llist_ref[t, k]]
            more = k + 1 < llen_ref[t]
            n, k = jnp.where(more, n, n + 1), jnp.where(more, k + 1, 2)
        return (n, k), tuple(todo)

    def near_first(todo, buf):
        for i in range(NEAR_UNROLL):
            buf[i] = near_product(sides[todo[3 * i + 1]], pool_ref[todo[3 * i + 2]])

    def near_last(todo, buf):
        parts = []
        for i in range(NEAR_UNROLL):
            parts.append(near_sums(buf.at[i], pool_ref[todo[3 * i + 2]], sub))
        for i in range(NEAR_UNROLL):
            near[todo[3 * i]] += parts[i]

    def near_body(carry):
        at, now = carry
        at, then = near_items(at)
        near_first(then, buf_b)
        near_last(now, buf_a)
        at, now = near_items(at)
        near_first(now, buf_a)
        near_last(then, buf_b)
        return at, now

    at, now = near_items((jnp.int32(0), jnp.int32(2)))
    near_first(now, buf_a)
    lax.while_loop(lambda carry: carry[1][0] < LEAVES, near_body, (at, now))

    def finish(g, carry):
        for i in range(4):
            t = 4 * g + i
            got = near[t]
            x = pool_ref[t][0:3]
            out_ref[t] = (3.0 * (x * got[6:7] - got[0:3]) - got[3:6]) + far_ref[t]
        return carry

    lax.fori_loop(0, LEAVES // 4, finish, 0)


def field(pool, sides, near, far, leaf_list, leaf_len):
    vmem = pl.BlockSpec(memory_space=pltpu.VMEM)
    smem = pl.BlockSpec(memory_space=pltpu.SMEM)
    return pl.pallas_call(
        field_kernel,
        out_shape=jax.ShapeDtypeStruct((LEAVES, 3, LANES), F32),
        in_specs=[vmem, vmem, vmem, vmem, smem, smem],
        out_specs=vmem,
        scratch_shapes=[
            pltpu.VMEM((LEAVES + 1, 8, LANES), F32),
            pltpu.SMEM((LEAVES + 8,), jnp.int32),
            pltpu.VMEM((NEAR_UNROLL, LANES, 2 * LANES), F32),
            pltpu.VMEM((NEAR_UNROLL, LANES, 2 * LANES), F32),
        ],
        compiler_params=pltpu.CompilerParams(vmem_limit_bytes=16 * 1024 * 1024),
        name="field",
    )(pool, sides, near, far, leaf_list, leaf_len)


def per_device(
    positions, moments, fwd_cells, fwd_leaves, fwd_counts, cell_list, cell_len, leaf_list, leaf_len
):
    pool, sides, near, far = exchange(
        positions, moments, fwd_leaves, fwd_counts, fwd_cells,
        leaf_list, leaf_len, cell_list, cell_len,
    )
    return field(pool, sides, near, far, leaf_list, leaf_len)


def solution(mesh):
    row = P("dom", None)
    cube = P("dom", None, None)
    return jax.shard_map(
        per_device,
        mesh=mesh,
        in_specs=(cube, cube, cube, cube, cube, row, P("dom"), row, P("dom")),
        out_specs=cube,
        check_vma=False,
    )
```

time: 126 us -> 84.3 us (0.67)
  the two profiles are of different devices: /device:TPU:50 before, /device:TPU:58 now
where the time goes in v3:
time: 84.3 us; the launch traced here: 83.9 us
  Pallas kernels  76.4 us (91%)
  local copies, waits for them, and re-layouts  7.55 us (9%)
    pallas_call x1, Pallas kernels, exchange(): pl.pallas_call(exchange_kernel, out_shape=(jax.ShapeDtypeStruct((LEAF_POO...  64.1 us
    pallas_call x1, Pallas kernels, field(): pl.pallas_call(field_kernel, out_shape=jax.ShapeDtypeStruct((LEAVES, 3, L...  12.3 us
    unnamed x12, local copies, waits for them, and re-layouts  6.9 us

profile of v3, /device:TPU:58, one launch (start us, length us, event | category | flops | bytes accessed | tf_op | source)
XLA Modules:
  0.0 83.9 jit_solution(14360977067268549738)
XLA Ops:
  0.0 0.7 copy.14.fc_ref
  0.7 0.7 copy.12.fl_ref
  1.4 0.8 copy.13.fn_ref
  2.1 0.8 copy.15.llist_ref
  2.9 1.0 %copy.10.pos_ref = f32[64,3,128]{2,1,0:T(4,128)S(1)} copy(f32[64,3,128]{2,0,1:T(8,128)} %param.9) | data formatting | bytes 196608 | tf_op args[0]
  3.9 1.0 %copy.11.mom_ref = f32[64,3,128]{2,1,0:T(4,128)S(1)} copy(f32[64,3,128]{2,0,1:T(8,128)} %param.10) | data formatting | bytes 196608 | tf_op args[1]
  4.8 0.0 copy-start
  4.9 0.7 copy-done
  5.6 0.0 copy-start.1
  5.6 0.7 copy-done.1
  6.3 0.0 copy-start.2
  6.3 0.7 copy-done.2
  6.9 64.1 %exchange.1 = (f32[244,8,128]{2,1,0:T(8,128)S(1)}, bf16[64,64,256]{2,1,0:T(8,128)(2,1)S(1)}, f32[64,8,128]{2,1,0:T(8,128)S(1)}, f32[64,3,128]{2,1,0:T(4,128)S(1)}) custom-call(f32[64,3,128]{2,1,0:T(4,128)S(1)} %copy.10.pos_ref, f32[64,3,128]{2,1,0:T(4,128)S(1)} %copy.11.mom_ref, s32[1,9,20]{2,1,0:T(8,128)S(1)} %copy.12.fl_ref, s32[1,9,2]{2,1,0:T(8,128)S(1)} %copy.13.fn_ref, ...), custom_call_target="tpu_custom_call" | custom-call | tf_op jit(solution)/shard_map/exchange/pallas_call | solution.py:451
  71.0 12.3 %field.1 = f32[64,3,128]{2,1,0:T(4,128)S(1)} custom-call(f32[244,8,128]{2,1,0:T(8,128)S(1)} %get-tuple-element.9.pool_ref, bf16[64,64,256]{2,1,0:T(8,128)(2,1)S(1)} %get-tuple-element.10.sides, f32[64,8,128]{2,1,0:T(8,128)S(1)} %get-tuple-element.11.near0, f32[64,3,128]{2,1,0:T(4,128)S(1)} %get-tuple-element.12.far_ref, s32[64,8]{1,0:T(8,128)S(1)} %copy.15.llist_ref, ...), custom_call_target="tpu_custom_call" | custom-call | tf_op jit(solution)/shard_map/field/pallas_call | solution.py:552
  83.3 0.6 copy.17
Async XLA Ops:
  4.8 0.8 copy-start
  5.6 0.7 copy-start.1
  6.3 0.7 copy-start.2

commit v4 on v3

--- a/solution.py
+++ b/solution.py
@@ -20,8 +20,8 @@
 WIDE = 128 + SECTIONS * CELL_SENDS
 LANES = 128
 N_DOM = 512
-NEAR_UNROLL = 4
-FAR_UNROLL = 2
+NEAR_UNROLL = 8
+FAR_UNROLL = 4
 
 
 def iota(shape, dim):
@@ -135,8 +135,8 @@
 
 
 def own_tile(pos_ref, mom_ref):
-    pos = [pos_ref[:, k, :] for k in range(3)]
-    mom = [mom_ref[:, k, :] for k in range(3)]
+    pos = [pos_ref[k] for k in range(3)]
+    mom = [mom_ref[k] for k in range(3)]
     cen = [jnp.sum(p, axis=1, keepdims=True) * (1.0 / LANES) for p in pos]
     tot = [jnp.sum(m, axis=1, keepdims=True) for m in mom]
     off = [pos[k] - cen[k] for k in range(3)]
@@ -228,26 +228,45 @@
     return (got[0:8] + got[8:16]) + more[0:8]
 
 
-def near_pass(count, first, last, buf_a, buf_b):
-    first(0, buf_a)
+def near_pass(steps, width, first, last, store, buf_a, buf_b):
+    def both(then, now, write, read):
+        parts = []
+        for i in range(width):
+            write[i] = first(then, i)
+            parts.append(last(now, i, read))
+        store(now, parts)
+
+    for i in range(width):
+        buf_a[i] = first(0, i)
 
     def body(i, carry):
-        g = 2 * i
-        first(g + 1, buf_b)
-        last(g, buf_a)
-        first(jnp.minimum(g + 2, count - 1), buf_a)
-        last(g + 1, buf_b)
+        both(2 * i + 1, 2 * i, buf_b, buf_a)
+        both(jnp.minimum(2 * i + 2, steps - 1), 2 * i + 1, buf_a, buf_b)
         return carry
 
-    lax.fori_loop(0, count // 2, body, 0)
+    lax.fori_loop(0, steps // 2, body, 0)
 
 
 def exchange_kernel(
-    pos_ref, mom_ref, fl_ref, fn_ref, fc_ref, llist_ref, llen_ref, clist_ref, clen_ref,
-    pool_ref, sides, near, far_ref,
+    pos_in, mom_in, fl_in, fn_in, fc_in, llist_in, llen_in, clist_in, clen_in,
+    pool_ref, sides, near, far_ref, llist_out, llen_out,
+    pos_ref, mom_ref, fl_ref, fn_ref, fc_ref, llist_ref, llen_ref, clist_ref, clen_ref, in_sem,
     split, feats, index, cindex, gath, pick, fsides, buf_a, buf_b, far_a, far_b,
     send_l, recv_l, send_c, recv_c, sl_sem, rl_sem, sc_sem, rc_sem,
 ):
+    loads = [
+        pltpu.make_async_copy(src, dst, in_sem.at[i])
+        for i, (src, dst) in enumerate(
+            (
+                (pos_in, pos_ref), (mom_in, mom_ref), (fl_in, fl_ref), (fn_in, fn_ref),
+                (fc_in, fc_ref), (llist_in, llist_ref), (llen_in, llen_ref),
+                (clist_in, clist_ref), (clen_in, clen_ref),
+                (llist_in, llist_out), (llen_in, llen_out),
+            )
+        )
+    ]
+    for load in loads:
+        load.start()
     me = lax.axis_index("dom")
     partners = []
     for b in range(SECTIONS):
@@ -258,13 +277,17 @@
         pl.semaphore_signal(
             barrier, inc=1, device_id=(other,), device_id_type=pl.DeviceIdType.MESH
         )
-    pool_ref[0:LEAVES, 0:3, :] = pos_ref[...]
-    pool_ref[0:LEAVES, 3:6, :] = mom_ref[...]
+    for load in loads:
+        load.wait()
+    for d in range(3):
+        pool_ref[0:LEAVES, d, :] = pos_ref[d]
+        pool_ref[0:LEAVES, 3 + d, :] = mom_ref[d]
 
     lane = iota((8, LANES), 1)
     sub = iota((8, LANES), 0)
     index[...] = jnp.full((16, LANES), -1, jnp.int32)
-    index[0:SECTIONS, 0:CELL_SENDS] = fc_ref[0]
+    for b in range(SECTIONS):
+        index[b : b + 1, 0:CELL_SENDS] = fc_ref[b]
     raw = index[...]
     index[...] = jnp.where(raw < OWN, raw, raw + (LANES - OWN))
     for half in range(2):
@@ -272,7 +295,6 @@
         cindex[:, half * 64 : half * 64 + 64] = jnp.where(
             rows < OWN, rows, rows + (LANES - OWN)
         )
-    pl.semaphore_wait(barrier, SECTIONS)
 
     def leaf_copy(b):
         return pltpu.make_async_remote_copy(
@@ -289,9 +311,9 @@
         )
 
     def send_leaves(b):
-        live = fn_ref[0, b, 1]
+        live = fn_ref[0, 1, b]
         for s in range(LEAF_SENDS):
-            block = pool_ref[fl_ref[0, b, s]][0:6]
+            block = pool_ref[fl_ref[b, 0, s]][0:6]
             send_l[b, 6 * s : 6 * s + 6, :] = jnp.where(s < live, block, 0.0)
         leaf_copy(b).start()
 
@@ -311,7 +333,7 @@
 
     def send_cells(b, msum):
         depth = LANES * ((b + 3) // 2)
-        wanted = jnp.where(lane[0:1] < fn_ref[0, b, 0], index[b : b + 1, :], -1)
+        wanted = jnp.where(lane[0:1] < fn_ref[0, 0, b], index[b : b + 1, :], -1)
         hot = jnp.where(iota((depth, LANES), 0) == wanted, 1.0, 0.0).astype(BF16)
         got = jnp.dot(split[:, 0:depth], hot, preferred_element_type=F32)
         got = (got[0:16] + got[16:32]) + got[32:48]
@@ -328,31 +350,36 @@
             part[0] * part[3] + part[1] * part[4] + part[2] * part[5]
         )
 
-    def prepare(t, carry):
-        block = pool_ref[t]
-        sides[t] = target_side(block, sub)
-        fsides[t] = far_side(block)
+    def prepare_near(g, carry):
+        for i in range(2):
+            t = 2 * g + i
+            sides[t] = target_side(pool_ref[t], sub)
+        return carry
+
+    def prepare_far(g, carry):
+        for i in range(2):
+            t = 2 * g + i
+            fsides[t] = far_side(pool_ref[t])
         return carry
 
     def near_source(t, k):
         if k == 0:
             return pool_ref[t]
-        return jnp.where(llen_ref[t] > 1, pool_ref[llist_ref[t, 1]], 0.0)
-
-    def near_steps(t0, count):
-        def first(g, buf):
+        return jnp.where(llen_ref[t] > 1, pool_ref[llist_ref[1, t]], 0.0)
+
+    def near_steps(t0, leaves):
+        def first(g, i):
+            t = t0 + 4 * g + i // 2
+            return near_product(sides[t], near_source(t, i % 2))
+
+        def last(g, i, buf):
+            return near_sums(buf.at[i], near_source(t0 + 4 * g + i // 2, i % 2), sub)
+
+        def store(g, parts):
             for i in range(4):
-                t = t0 + 2 * g + i // 2
-                buf[i] = near_product(sides[t], near_source(t, i % 2))
-
-        def last(g, buf):
-            for i in range(2):
-                t = t0 + 2 * g + i
-                near[t] = near_sums(buf.at[2 * i], near_source(t, 0), sub) + near_sums(
-                    buf.at[2 * i + 1], near_source(t, 1), sub
-                )
-
-        near_pass(count // 2, first, last, buf_a, buf_b)
+                near[t0 + 4 * g + i] = parts[2 * i] + parts[2 * i + 1]
+
+        near_pass(leaves // 4, 8, first, last, store, buf_a, buf_b)
 
     def wanted_cells(i):
         row = cindex[pl.ds(i, 1), :]
@@ -362,55 +389,78 @@
 
     old = LANES + (SECTIONS - 1) * CELL_SENDS
 
-    def gather_old(g, carry):
-        for j in range(2):
-            i = 2 * g + j
-            hot = jnp.where(iota((old, LANES), 0) == wanted_cells(i), 1.0, 0.0).astype(BF16)
-            gath[i] = jnp.dot(feats[:, 0:old], hot, preferred_element_type=F32)
-        return carry
-
-    def far_first(g, buf):
+    def gather(low, high):
+        def body(g, carry):
+            for j in range(4):
+                i = 4 * g + j
+                spot = iota((high - low, LANES), 0) + low
+                hot = jnp.where(spot == wanted_cells(i), 1.0, 0.0).astype(BF16)
+                got = jnp.dot(feats[:, low:high], hot, preferred_element_type=F32)
+                gath[i] = got if low == 0 else gath[i] + got
+            return carry
+
+        lax.fori_loop(0, 8, body, 0)
+
+    def far_first(g, j):
+        i = FAR_UNROLL * g + j
+        hot = jnp.where(iota((64, LANES), 0) + old == wanted_cells(i), 1.0, 0.0).astype(BF16)
+        picked = gath[i] + jnp.dot(feats[:, old : old + 64], hot, preferred_element_type=F32)
+        pick[i] = picked
+        return jnp.concatenate(
+            [
+                far_product(fsides[i], picked[:, 0:64]),
+                far_product(fsides[i + 32], pltpu.roll(picked, 64, 1)[:, 0:64]),
+            ],
+            axis=0,
+        )
+
+    def far_last(g, j, buf):
+        i = FAR_UNROLL * g + j
+        parts = []
+        for half in range(2):
+            picked = pick[i, 0:32]
+            if half:
+                picked = pltpu.roll(picked, 64, 1)
+            parts.append(
+                far_sums(
+                    buf[j, 64 * half : 64 * half + 64], picked[:, 0:64], pool_ref[i + 32 * half]
+                )
+            )
+        return parts
+
+    def far_store(g, parts, unif):
         for j in range(FAR_UNROLL):
-            i = FAR_UNROLL * g + j
-            hot = jnp.where(
-                iota((LANES, LANES), 0) + old == wanted_cells(i), 1.0, 0.0
-            ).astype(BF16)
-            picked = gath[i] + jnp.dot(
-                feats[:, old : old + LANES], hot, preferred_element_type=F32
-            )
-            pick[i] = picked
-            buf[2 * j] = far_product(fsides[i], picked[:, 0:64])
-            buf[2 * j + 1] = far_product(fsides[i + 32], pltpu.roll(picked, 64, 1)[:, 0:64])
-
-    def far_last(g, buf, unif):
-        for j in range(FAR_UNROLL):
-            i = FAR_UNROLL * g + j
             for half in range(2):
-                picked = pick[i, 0:32]
-                if half:
-                    picked = pltpu.roll(picked, 64, 1)
-                t = i + 32 * half
-                parts = far_sums(buf[2 * j + half], picked[:, 0:64], pool_ref[t])
+                t = FAR_UNROLL * g + j + 32 * half
                 for d in range(3):
-                    far_ref[t, d : d + 1, :] = parts[d] + unif[d]
+                    far_ref[d, pl.ds(t, 1), :] = parts[j][half][d] + unif[d]
 
     def beside(b):
         if b == 0:
-            finish_leaves(0, LEAVES)
-            lax.fori_loop(0, LEAVES, prepare, 0)
-        elif b < 5:
-            near_steps(16 * (b - 1), 16)
+            lax.fori_loop(0, LEAVES // 2, prepare_near, 0)
+        elif b == 1:
+            near_steps(0, 16)
+        elif b == 2:
+            near_steps(16, 16)
+        elif b == 3:
+            near_steps(32, 32)
+        elif b == 4:
+            lax.fori_loop(0, LEAVES // 2, prepare_far, 0)
+        elif b == 5:
+            gather(0, 384)
         elif b == SECTIONS - 1:
-            lax.fori_loop(0, 16, gather_old, 0)
-
-    send_leaves(0)
+            gather(384, old)
+
     tile, sums = own_tile(pos_ref, mom_ref)
     msum = jnp.zeros((8, LANES), F32)
     for j in range(3):
         msum = jnp.where((sub == 7) & (lane == j), sums[j], msum)
     take_split(tile, 0)
+    finish_leaves(0, LEAVES)
+    take_features(tile, 0)
+    pl.semaphore_wait(barrier, SECTIONS)
+    send_leaves(0)
     send_cells(0, msum)
-    take_features(tile, 0)
     beside(0)
     for b in range(SECTIONS):
         first = LEAVES + b * LEAF_SENDS
@@ -435,7 +485,8 @@
     scaled = msum * (-DEMAG / (N_DOM * LEAVES))
     unif = [jnp.broadcast_to(scaled[7:8, j : j + 1], (1, LANES)) for j in range(3)]
     near_pass(
-        32 // FAR_UNROLL, far_first, lambda g, buf: far_last(g, buf, unif), far_a, far_b
+        32 // FAR_UNROLL, FAR_UNROLL, far_first, far_last,
+        lambda g, parts: far_store(g, parts, unif), far_a, far_b,
     )
     for b in range(SECTIONS):
         leaf_copy(b).wait_send()
@@ -446,7 +497,7 @@
     positions, moments, fwd_leaves, fwd_counts, fwd_cells, leaf_list, leaf_len, cell_list, cell_len
 ):
     vmem = pl.BlockSpec(memory_space=pltpu.VMEM)
-    smem = pl.BlockSpec(memory_space=pltpu.SMEM)
+    hbm = pl.BlockSpec(memory_space=pltpu.MemorySpace.HBM)
     dma = pltpu.SemaphoreType.DMA((SECTIONS,))
     return pl.pallas_call(
         exchange_kernel,
@@ -454,11 +505,23 @@
             jax.ShapeDtypeStruct((LEAF_POOL, 8, LANES), F32),
             jax.ShapeDtypeStruct((LEAVES, 64, 2 * LANES), BF16),
             jax.ShapeDtypeStruct((LEAVES, 8, LANES), F32),
-            jax.ShapeDtypeStruct((LEAVES, 3, LANES), F32),
+            jax.ShapeDtypeStruct((3, LEAVES, LANES), F32),
+            jax.ShapeDtypeStruct((8, LEAVES), jnp.int32),
+            jax.ShapeDtypeStruct((LEAVES,), jnp.int32),
         ),
-        in_specs=[vmem, vmem, smem, smem, vmem, smem, smem, vmem, smem],
-        out_specs=(vmem, vmem, vmem, vmem),
+        in_specs=[hbm] * 9,
+        out_specs=(vmem,) * 6,
         scratch_shapes=[
+            pltpu.VMEM((3, LEAVES, LANES), F32),
+            pltpu.VMEM((3, LEAVES, LANES), F32),
+            pltpu.SMEM((SECTIONS, 1, LEAF_SENDS), jnp.int32),
+            pltpu.SMEM((1, 2, SECTIONS), jnp.int32),
+            pltpu.VMEM((SECTIONS, 1, CELL_SENDS), jnp.int32),
+            pltpu.SMEM((8, LEAVES), jnp.int32),
+            pltpu.SMEM((LEAVES,), jnp.int32),
+            pltpu.VMEM((LEAVES, 64), jnp.int32),
+            pltpu.SMEM((LEAVES,), jnp.int32),
+            pltpu.SemaphoreType.DMA((11,)),
             pltpu.VMEM((48, WIDE + 64), BF16),
             pltpu.VMEM((64, WIDE + 64), BF16),
             pltpu.VMEM((16, LANES), jnp.int32),
@@ -466,10 +529,10 @@
             pltpu.VMEM((32, 64, LANES), F32),
             pltpu.VMEM((32, 64, LANES), F32),
             pltpu.VMEM((LEAVES, 112, 3 * LANES), BF16),
-            pltpu.VMEM((4, LANES, 2 * LANES), F32),
-            pltpu.VMEM((4, LANES, 2 * LANES), F32),
-            pltpu.VMEM((2 * FAR_UNROLL, 64, 3 * LANES), F32),
-            pltpu.VMEM((2 * FAR_UNROLL, 64, 3 * LANES), F32),
+            pltpu.VMEM((8, LANES, 2 * LANES), F32),
+            pltpu.VMEM((8, LANES, 2 * LANES), F32),
+            pltpu.VMEM((FAR_UNROLL, LANES, 3 * LANES), F32),
+            pltpu.VMEM((FAR_UNROLL, LANES, 3 * LANES), F32),
             pltpu.VMEM((SECTIONS, 6 * LEAF_SENDS, LANES), F32),
             pltpu.VMEM((SECTIONS, 6 * LEAF_SENDS, LANES), F32),
             pltpu.VMEM((SECTIONS, 8, LANES), F32),
@@ -481,8 +544,13 @@
         ),
         name="exchange",
     )(
-        positions, moments, fwd_leaves, fwd_counts, fwd_cells,
-        leaf_list, leaf_len, cell_list, cell_len,
+        *(
+            pltpu.with_memory_space_constraint(x, pltpu.MemorySpace.HBM)
+            for x in (
+                positions, moments, fwd_leaves, fwd_counts, fwd_cells,
+                leaf_list, leaf_len, cell_list, cell_len,
+            )
+        )
     )
 
 
@@ -497,7 +565,6 @@
 
     busy = lax.fori_loop(0, LEAVES, collect, 0)
     near[0:LEAVES] = near0[...]
-    near[LEAVES] = jnp.zeros((8, LANES), F32)
 
     def near_items(at):
         n, k = at
@@ -505,45 +572,45 @@
         for _ in range(NEAR_UNROLL):
             t = todo_ref[jnp.minimum(n, LEAVES - 1)]
             t = jnp.where(n < busy, t, 0)
-            todo += [jnp.where(n < busy, t, LEAVES), t, llist_ref[t, k]]
+            todo += [jnp.where(n < busy, t, LEAVES), t, llist_ref[k, t], k]
             more = k + 1 < llen_ref[t]
             n, k = jnp.where(more, n, n + 1), jnp.where(more, k + 1, 2)
         return (n, k), tuple(todo)
 
-    def near_first(todo, buf):
-        for i in range(NEAR_UNROLL):
-            buf[i] = near_product(sides[todo[3 * i + 1]], pool_ref[todo[3 * i + 2]])
-
-    def near_last(todo, buf):
+    def near_both(then, now, write, read, acc):
         parts = []
         for i in range(NEAR_UNROLL):
-            parts.append(near_sums(buf.at[i], pool_ref[todo[3 * i + 2]], sub))
+            write[i] = near_product(sides[then[4 * i + 1]], pool_ref[then[4 * i + 2]])
+            parts.append(near_sums(read.at[i], pool_ref[now[4 * i + 2]], sub))
         for i in range(NEAR_UNROLL):
-            near[todo[3 * i]] += parts[i]
+            acc = jnp.where(now[4 * i + 3] == 2, near0[now[4 * i + 1]], acc) + parts[i]
+            near[now[4 * i]] = acc
+        return acc
 
     def near_body(carry):
-        at, now = carry
-        at, then = near_items(at)
-        near_first(then, buf_b)
-        near_last(now, buf_a)
-        at, now = near_items(at)
-        near_first(now, buf_a)
-        near_last(then, buf_b)
-        return at, now
+        at, now, then, acc = carry
+        at, later = near_items(at)
+        acc = near_both(then, now, buf_b, buf_a, acc)
+        at, last = near_items(at)
+        acc = near_both(later, then, buf_a, buf_b, acc)
+        return at, later, last, acc
 
     at, now = near_items((jnp.int32(0), jnp.int32(2)))
-    near_first(now, buf_a)
-    lax.while_loop(lambda carry: carry[1][0] < LEAVES, near_body, (at, now))
-
-    def finish(g, carry):
-        for i in range(4):
-            t = 4 * g + i
-            got = near[t]
-            x = pool_ref[t][0:3]
-            out_ref[t] = (3.0 * (x * got[6:7] - got[0:3]) - got[3:6]) + far_ref[t]
-        return carry
-
-    lax.fori_loop(0, LEAVES // 4, finish, 0)
+    at, then = near_items(at)
+    for i in range(NEAR_UNROLL):
+        buf_a[i] = near_product(sides[now[4 * i + 1]], pool_ref[now[4 * i + 2]])
+    lax.while_loop(
+        lambda carry: carry[1][0] < LEAVES,
+        near_body,
+        (at, now, then, jnp.zeros((8, LANES), F32)),
+    )
+
+    for d in range(3):
+        got = near[0:LEAVES, d, :]
+        x = pool_ref[0:LEAVES, d, :]
+        out_ref[d] = (
+            3.0 * (x * near[0:LEAVES, 6, :] - got) - near[0:LEAVES, 3 + d, :] + far_ref[d]
+        )
 
 
 def field(pool, sides, near, far, leaf_list, leaf_len):
@@ -551,7 +618,7 @@
     smem = pl.BlockSpec(memory_space=pltpu.SMEM)
     return pl.pallas_call(
         field_kernel,
-        out_shape=jax.ShapeDtypeStruct((LEAVES, 3, LANES), F32),
+        out_shape=jax.ShapeDtypeStruct((3, LEAVES, LANES), F32),
         in_specs=[vmem, vmem, vmem, vmem, smem, smem],
         out_specs=vmem,
         scratch_shapes=[
@@ -568,11 +635,12 @@
 def per_device(
     positions, moments, fwd_cells, fwd_leaves, fwd_counts, cell_list, cell_len, leaf_list, leaf_len
 ):
-    pool, sides, near, far = exchange(
-        positions, moments, fwd_leaves, fwd_counts, fwd_cells,
-        leaf_list, leaf_len, cell_list, cell_len,
-    )
-    return field(pool, sides, near, far, leaf_list, leaf_len)
+    swap = lambda x: jnp.transpose(x, (1, 0, 2))
+    pool, sides, near, far, lists, lens = exchange(
+        swap(positions), swap(moments), swap(fwd_leaves), jnp.transpose(fwd_counts, (0, 2, 1)),
+        swap(fwd_cells), leaf_list.T, leaf_len, cell_list, cell_len,
+    )
+    return swap(field(pool, sides, near, far, lists, lens))
 
 
 def solution(mesh):

time: 84.3 us -> 72.7 us (0.86)
  the two profiles are of different devices: /device:TPU:58 before, /device:TPU:56 now
where the time goes in v4:
time: 72.7 us; the launch traced here: 72.6 us
  Pallas kernels  72.6 us (100%)
    pallas_call x1, Pallas kernels, exchange(): pl.pallas_call(exchange_kernel, out_shape=(jax.ShapeDtypeStruct((LEAF_POO...  62.7 us
    pallas_call x1, Pallas kernels, field(): pl.pallas_call(field_kernel, out_shape=jax.ShapeDtypeStruct((3, LEAVES, L...  9.84 us

profile of v4, /device:TPU:56, one launch (start us, length us, event | category | flops | bytes accessed | tf_op | source)
XLA Modules:
  0.0 72.6 jit_solution(5851617315767204946)
XLA Ops:
  0.0 62.7 %exchange.1 = (f32[244,8,128]{2,1,0:T(8,128)S(1)}, bf16[64,64,256]{2,1,0:T(8,128)(2,1)S(1)}, f32[64,8,128]{2,1,0:T(8,128)S(1)}, f32[3,64,128]{2,1,0:T(8,128)S(1)}, s32[8,64]{1,0:T(8,128)S(1)}, /*index=5*/s32[64]{0:T(128)S(1)}) custom-call(f32[3,64,128]{2,1,0:T(8,128)} %bitcast.7, f32[3,64,128]{2,1,0:T(8,128)} %bitcast.8, s32[9,1,20]{2,1,0:T(1,128)} %bitcast.9, ...), custom_call_target="tpu_custom_call" | custom-call | tf_op jit(solution)/shard_map/exchange/pallas_call | solution.py:502
  62.7 9.8 %field.1 = f32[3,64,128]{2,1,0:T(8,128)} custom-call(f32[244,8,128]{2,1,0:T(8,128)S(1)} %get-tuple-element.11.pool_ref, bf16[64,64,256]{2,1,0:T(8,128)(2,1)S(1)} %get-tuple-element.12.sides, f32[64,8,128]{2,1,0:T(8,128)S(1)} %get-tuple-element.13.near0, f32[3,64,128]{2,1,0:T(8,128)S(1)} %get-tuple-element.14.far_ref, ...), custom_call_target="tpu_custom_call" | custom-call | tf_op jit(solution)/shard_map/field/pallas_call | solution.py:619

commit v5 on v4

--- a/solution.py
+++ b/solution.py
@@ -21,6 +21,8 @@
 LANES = 128
 N_DOM = 512
 NEAR_UNROLL = 8
+LEAD = 3
+HELD = (LEAVES + 6 * LEAF_SENDS, LEAVES + 7 * LEAF_SENDS)
 FAR_UNROLL = 4
 
 
@@ -52,10 +54,10 @@
     )
     rest = jnp.concatenate(
         [
-            c[0] * c[0] + c[1] * c[1] + c[2] * c[2] + 1.0,
+            c[0] * c[0] + c[1] * c[1] + c[2] * c[2],
             -(tot[0] * c[0] + tot[1] * c[1] + tot[2] * c[2])
             - (sec(0, 0) + sec(1, 1) + sec(2, 2)),
-            c[0] * turn[0] + c[1] * turn[1] + c[2] * turn[2],
+            2.5 * (c[0] * turn[0] + c[1] * turn[1] + c[2] * turn[2]),
         ],
         axis=0,
     )
@@ -71,9 +73,9 @@
     along = jnp.concatenate([none(3), x3, none(10)], axis=0)
     bend = jnp.concatenate(
         [
-            none(6), x[0] * x[0], x[1] * x[1], x[2] * x[2],
-            2.0 * (x[0] * x[1]), 2.0 * (x[0] * x[2]), 2.0 * (x[1] * x[2]),
-            -2.0 * x3, none(1),
+            none(6), 2.5 * (x[0] * x[0]), 2.5 * (x[1] * x[1]), 2.5 * (x[2] * x[2]),
+            5.0 * (x[0] * x[1]), 5.0 * (x[0] * x[2]), 5.0 * (x[1] * x[2]),
+            -5.0 * x3, none(1),
         ],
         axis=0,
     )
@@ -81,30 +83,36 @@
     cols = []
     for i, part in enumerate((quad, along, bend)):
         p0, p1, p2 = pieces(part)
-        ones = jnp.where((sub < 9) & (lax.rem(sub, 3) == i), 1.0, 0.0)
+        ones = jnp.where((sub < 9 + (i == 0)) & (lax.rem(sub, 3) == i), 1.0, 0.0)
         cols.append(jnp.concatenate([p0, p1, p2, p0, p1, p0, ones], axis=0).astype(BF16))
     return jnp.concatenate(cols, axis=1)
 
 
 def far_product(side, picked):
     a0, a1, a2, rest = picked[0:16], picked[16:32], picked[32:48], picked[48:64]
+    rest = jnp.where(iota((16, 64), 0) == 9, 1.0, rest)
     stack = jnp.concatenate([a0, a0, a0, a1, a1, a2, rest], axis=0).astype(BF16)
     return lax.dot_general(stack, side, (((0,), (0,)), ((), ())), preferred_element_type=F32)
 
 
 def far_sums(both, picked, block):
-    quad = jnp.maximum(both[:, 0:LANES], 1.0)
-    inv = lax.rsqrt(quad)
-    inv2 = inv * inv
-    inv3 = inv2 * inv
-    inv5 = 3.0 * (inv3 * inv2)
-    inv7 = 2.5 * (inv5 * inv2)
-    coef = both[:, LANES : 2 * LANES] * inv5 + both[:, 2 * LANES :] * inv7
+    weights = [[], [], []]
+    for c in range(4):
+        rows = slice(16 * c, 16 * c + 16)
+        inv = lax.rsqrt(both[rows, 0:LANES])
+        inv2 = inv * inv
+        inv3 = inv2 * inv
+        inv5 = inv3 * inv2
+        coef = (both[rows, LANES : 2 * LANES] + both[rows, 2 * LANES :] * inv2) * inv5
+        for out, weight in zip(weights, (coef, inv3, inv5)):
+            high = weight.astype(BF16)
+            low = (weight - high.astype(F32)).astype(BF16)
+            out.append(jnp.concatenate([high, low], axis=1))
     sub = iota((16, 64), 0)
 
     def lefts(part, one):
         first = jnp.where(sub < 3, part, jnp.where(sub == 3, one, 0.0))
-        second = jnp.where(sub < 3, pltpu.roll(part, 13, 0), 0.0)
+        second = jnp.where((sub >= 10) & (sub < 13), pltpu.roll(part, 7, 0), 0.0)
         third = jnp.where(
             sub < 3,
             -pltpu.roll(part, 4, 0),
@@ -113,15 +121,9 @@
         return first, second, third
 
     total = None
-    for weight, high_l, low_l in zip(
-        (coef, inv3, inv5), lefts(picked[0:16], 1.0), lefts(picked[16:32], 0.0)
-    ):
-        high = weight.astype(BF16)
-        low = (weight - high.astype(F32)).astype(BF16)
+    for weight, high_l, low_l in zip(weights, lefts(picked[0:16], 1.0), lefts(picked[16:32], 0.0)):
         left = jnp.concatenate([high_l, low_l], axis=0).astype(BF16)
-        part = jnp.dot(
-            left, jnp.concatenate([high, low], axis=1), preferred_element_type=F32
-        )
+        part = jnp.dot(left, jnp.concatenate(weight, axis=0), preferred_element_type=F32)
         total = part if total is None else total + part
     got = (total[0:16, 0:LANES] + total[16:32, 0:LANES]) + total[0:16, LANES:]
     x = [block[d : d + 1] for d in range(3)]
@@ -131,7 +133,10 @@
         q[3] * x[0] + q[1] * x[1] + q[5] * x[2],
         q[4] * x[0] + q[5] * x[1] + q[2] * x[2],
     ]
-    return [x[d] * got[3:4] - got[d : d + 1] - turn[d] for d in range(3)]
+    return [
+        3.0 * (x[d] * got[3:4] - got[d : d + 1] - turn[d]) - got[10 + d : 11 + d]
+        for d in range(3)
+    ]
 
 
 def own_tile(pos_ref, mom_ref):
@@ -231,13 +236,15 @@
 def near_pass(steps, width, first, last, store, buf_a, buf_b):
     def both(then, now, write, read):
         parts = []
-        for i in range(width):
-            write[i] = first(then, i)
-            parts.append(last(now, i, read))
+        for i in range(width + LEAD):
+            if i < width:
+                first(then, i, write)
+            if i >= LEAD:
+                parts.append(last(now, i - LEAD, read))
         store(now, parts)
 
     for i in range(width):
-        buf_a[i] = first(0, i)
+        first(0, i, buf_a)
 
     def body(i, carry):
         both(2 * i + 1, 2 * i, buf_b, buf_a)
@@ -251,7 +258,7 @@
     pos_in, mom_in, fl_in, fn_in, fc_in, llist_in, llen_in, clist_in, clen_in,
     pool_ref, sides, near, far_ref, llist_out, llen_out,
     pos_ref, mom_ref, fl_ref, fn_ref, fc_ref, llist_ref, llen_ref, clist_ref, clen_ref, in_sem,
-    split, feats, index, cindex, gath, pick, fsides, buf_a, buf_b, far_a, far_b,
+    split, feats, index, cindex, gath, fsides, buf_a, buf_b, far_a, far_b, pick_a, pick_b, kept_a, kept_b,
     send_l, recv_l, send_c, recv_c, sl_sem, rl_sem, sc_sem, rc_sem,
 ):
     loads = [
@@ -362,24 +369,36 @@
             fsides[t] = far_side(pool_ref[t])
         return carry
 
-    def near_source(t, k):
+    def near_source(t, k, held):
         if k == 0:
             return pool_ref[t]
-        return jnp.where(llen_ref[t] > 1, pool_ref[llist_ref[1, t]], 0.0)
-
-    def near_steps(t0, leaves):
-        def first(g, i):
-            t = t0 + 4 * g + i // 2
-            return near_product(sides[t], near_source(t, i % 2))
+        src = llist_ref[k, t]
+        use = llen_ref[t] > k
+        if k > 1:
+            use = use & (src < held)
+        return jnp.where(use, pool_ref[src], 0.0)
+
+    def near_steps(t0, leaves, places, held=0):
+        n = len(places)
+
+        def spot(g, i):
+            return t0 + 8 // n * g + i // n, places[i % n]
+
+        def first(g, i, buf):
+            t, k = spot(g, i)
+            buf[i] = near_product(sides[t], near_source(t, k, held))
 
         def last(g, i, buf):
-            return near_sums(buf.at[i], near_source(t0 + 4 * g + i // 2, i % 2), sub)
+            t, k = spot(g, i)
+            return near_sums(buf.at[i], near_source(t, k, held), sub)
 
         def store(g, parts):
-            for i in range(4):
-                near[t0 + 4 * g + i] = parts[2 * i] + parts[2 * i + 1]
-
-        near_pass(leaves // 4, 8, first, last, store, buf_a, buf_b)
+            for i in range(0, 8, n):
+                t, k = spot(g, i)
+                got = parts[i] if n == 1 else parts[i] + parts[i + 1]
+                near[t] = got if k == 0 else near[t] + got
+
+        near_pass(leaves * n // 8, 8, first, last, store, buf_a, buf_b)
 
     def wanted_cells(i):
         row = cindex[pl.ds(i, 1), :]
@@ -401,32 +420,27 @@
 
         lax.fori_loop(0, 8, body, 0)
 
-    def far_first(g, j):
+    def far_pick(g, j, buf):
         i = FAR_UNROLL * g + j
         hot = jnp.where(iota((64, LANES), 0) + old == wanted_cells(i), 1.0, 0.0).astype(BF16)
         picked = gath[i] + jnp.dot(feats[:, old : old + 64], hot, preferred_element_type=F32)
-        pick[i] = picked
-        return jnp.concatenate(
-            [
-                far_product(fsides[i], picked[:, 0:64]),
-                far_product(fsides[i + 32], pltpu.roll(picked, 64, 1)[:, 0:64]),
-            ],
-            axis=0,
-        )
+        buf[2 * j] = picked
+        buf[2 * j + 1] = pltpu.roll(picked, 64, 1)
+
+    def far_middle(g, j, read, buf):
+        both, kept = buf
+        for h in range(2):
+            part = read[2 * j + h]
+            kept[2 * j + h] = part[0:32]
+            both[2 * j + h] = far_product(fsides[FAR_UNROLL * g + j + 32 * h], part[:, 0:64])
 
     def far_last(g, j, buf):
         i = FAR_UNROLL * g + j
-        parts = []
-        for half in range(2):
-            picked = pick[i, 0:32]
-            if half:
-                picked = pltpu.roll(picked, 64, 1)
-            parts.append(
-                far_sums(
-                    buf[j, 64 * half : 64 * half + 64], picked[:, 0:64], pool_ref[i + 32 * half]
-                )
-            )
-        return parts
+        both, kept = buf
+        return [
+            far_sums(both.at[2 * j + h], kept[2 * j + h][:, 0:64], pool_ref[i + 32 * h])
+            for h in range(2)
+        ]
 
     def far_store(g, parts, unif):
         for j in range(FAR_UNROLL):
@@ -439,28 +453,33 @@
         if b == 0:
             lax.fori_loop(0, LEAVES // 2, prepare_near, 0)
         elif b == 1:
-            near_steps(0, 16)
+            near_steps(0, 16, (0, 1))
         elif b == 2:
-            near_steps(16, 16)
+            near_steps(16, 16, (0, 1))
         elif b == 3:
-            near_steps(32, 32)
+            near_steps(32, 32, (0, 1))
         elif b == 4:
             lax.fori_loop(0, LEAVES // 2, prepare_far, 0)
         elif b == 5:
             gather(0, 384)
-        elif b == SECTIONS - 1:
+        elif b == 6:
+            near_steps(0, LEAVES, (2,), HELD[0])
+        elif b == 7:
+            near_steps(0, 32, (3,), HELD[1])
+        elif b == 8:
+            near_steps(32, 32, (3,), HELD[1])
             gather(384, old)
 
+    pl.semaphore_wait(barrier, SECTIONS)
+    send_leaves(0)
     tile, sums = own_tile(pos_ref, mom_ref)
     msum = jnp.zeros((8, LANES), F32)
     for j in range(3):
         msum = jnp.where((sub == 7) & (lane == j), sums[j], msum)
     take_split(tile, 0)
+    send_cells(0, msum)
     finish_leaves(0, LEAVES)
     take_features(tile, 0)
-    pl.semaphore_wait(barrier, SECTIONS)
-    send_leaves(0)
-    send_cells(0, msum)
     beside(0)
     for b in range(SECTIONS):
         first = LEAVES + b * LEAF_SENDS
@@ -484,10 +503,29 @@
             beside(b + 1)
     scaled = msum * (-DEMAG / (N_DOM * LEAVES))
     unif = [jnp.broadcast_to(scaled[7:8, j : j + 1], (1, LANES)) for j in range(3)]
-    near_pass(
-        32 // FAR_UNROLL, FAR_UNROLL, far_first, far_last,
-        lambda g, parts: far_store(g, parts, unif), far_a, far_b,
-    )
+    steps = 32 // FAR_UNROLL
+    capped = lambda g: jnp.minimum(g, steps - 1)
+
+    def far_round(g, pick_w, pick_r, far_w, far_r):
+        parts = []
+        for j in range(FAR_UNROLL):
+            far_pick(capped(g + 2), j, pick_w)
+            far_middle(capped(g + 1), j, pick_r, far_w)
+            parts.append(far_last(g, j, far_r))
+        far_store(g, parts, unif)
+
+    for j in range(FAR_UNROLL):
+        far_pick(0, j, pick_a)
+        far_pick(1, j, pick_b)
+    for j in range(FAR_UNROLL):
+        far_middle(0, j, pick_a, (far_a, kept_a))
+
+    def far_body(i, carry):
+        far_round(2 * i, pick_a, pick_b, (far_b, kept_b), (far_a, kept_a))
+        far_round(2 * i + 1, pick_b, pick_a, (far_a, kept_a), (far_b, kept_b))
+        return carry
+
+    lax.fori_loop(0, steps // 2, far_body, 0)
     for b in range(SECTIONS):
         leaf_copy(b).wait_send()
         cell_copy(b).wait_send()
@@ -527,12 +565,15 @@
             pltpu.VMEM((16, LANES), jnp.int32),
             pltpu.VMEM((32, LANES), jnp.int32),
             pltpu.VMEM((32, 64, LANES), F32),
-            pltpu.VMEM((32, 64, LANES), F32),
             pltpu.VMEM((LEAVES, 112, 3 * LANES), BF16),
             pltpu.VMEM((8, LANES, 2 * LANES), F32),
             pltpu.VMEM((8, LANES, 2 * LANES), F32),
-            pltpu.VMEM((FAR_UNROLL, LANES, 3 * LANES), F32),
-            pltpu.VMEM((FAR_UNROLL, LANES, 3 * LANES), F32),
+            pltpu.VMEM((2 * FAR_UNROLL, 64, 3 * LANES), F32),
+            pltpu.VMEM((2 * FAR_UNROLL, 64, 3 * LANES), F32),
+            pltpu.VMEM((2 * FAR_UNROLL, 64, LANES), F32),
+            pltpu.VMEM((2 * FAR_UNROLL, 64, LANES), F32),
+            pltpu.VMEM((2 * FAR_UNROLL, 32, LANES), F32),
+            pltpu.VMEM((2 * FAR_UNROLL, 32, LANES), F32),
             pltpu.VMEM((SECTIONS, 6 * LEAF_SENDS, LANES), F32),
             pltpu.VMEM((SECTIONS, 6 * LEAF_SENDS, LANES), F32),
             pltpu.VMEM((SECTIONS, 8, LANES), F32),
@@ -555,36 +596,51 @@
 
 
 def field_kernel(
-    pool_ref, sides, near0, far_ref, llist_ref, llen_ref, out_ref, near, todo_ref, buf_a, buf_b
+    pool_ref, sides, near0, far_ref, llist_ref, llen_ref, out_ref, near, todo_ref, from_ref,
+    buf_a, buf_b
 ):
     sub = iota((8, LANES), 0)
 
-    def collect(t, count):
-        todo_ref[count] = t
-        return jnp.where(llen_ref[t] > 2, count + 1, count)
-
-    busy = lax.fori_loop(0, LEAVES, collect, 0)
+    busy = jnp.int32(0)
+    for t in range(LEAVES):
+        size = llen_ref[t]
+        late = (size > 2) & (llist_ref[2, t] >= HELD[0])
+        again = (size > 3) & (llist_ref[3, t] >= HELD[1])
+        start = jnp.where(late, 2, jnp.where(again, 3, 4))
+        todo_ref[busy] = t
+        from_ref[busy] = start
+        busy = busy + (start < size).astype(jnp.int32)
     near[0:LEAVES] = near0[...]
 
     def near_items(at):
         n, k = at
         todo = []
         for _ in range(NEAR_UNROLL):
-            t = todo_ref[jnp.minimum(n, LEAVES - 1)]
-            t = jnp.where(n < busy, t, 0)
-            todo += [jnp.where(n < busy, t, LEAVES), t, llist_ref[k, t], k]
+            here = jnp.minimum(n, LEAVES - 1)
+            t = jnp.where(n < busy, todo_ref[here], 0)
+            start = from_ref[here]
+            k = jnp.where(k < 0, jnp.where(n < busy, start, 2), k)
+            src = llist_ref[k, t]
+            used = (k != 3) | (src >= HELD[1])
+            todo += [
+                jnp.where(n < busy, t, LEAVES), t, src,
+                (k == start).astype(jnp.int32), used.astype(jnp.int32),
+            ]
             more = k + 1 < llen_ref[t]
-            n, k = jnp.where(more, n, n + 1), jnp.where(more, k + 1, 2)
+            n, k = jnp.where(more, n, n + 1), jnp.where(more, k + 1, -1)
         return (n, k), tuple(todo)
+
+    def source(todo, i):
+        return jnp.where(todo[5 * i + 4] > 0, pool_ref[todo[5 * i + 2]], 0.0)
 
     def near_both(then, now, write, read, acc):
         parts = []
         for i in range(NEAR_UNROLL):
-            write[i] = near_product(sides[then[4 * i + 1]], pool_ref[then[4 * i + 2]])
-            parts.append(near_sums(read.at[i], pool_ref[now[4 * i + 2]], sub))
+            write[i] = near_product(sides[then[5 * i + 1]], source(then, i))
+            parts.append(near_sums(read.at[i], source(now, i), sub))
         for i in range(NEAR_UNROLL):
-            acc = jnp.where(now[4 * i + 3] == 2, near0[now[4 * i + 1]], acc) + parts[i]
-            near[now[4 * i]] = acc
+            acc = jnp.where(now[5 * i + 3] > 0, near0[now[5 * i + 1]], acc) + parts[i]
+            near[now[5 * i]] = acc
         return acc
 
     def near_body(carry):
@@ -595,10 +651,10 @@
         acc = near_both(later, then, buf_a, buf_b, acc)
         return at, later, last, acc
 
-    at, now = near_items((jnp.int32(0), jnp.int32(2)))
+    at, now = near_items((jnp.int32(0), jnp.int32(-1)))
     at, then = near_items(at)
     for i in range(NEAR_UNROLL):
-        buf_a[i] = near_product(sides[now[4 * i + 1]], pool_ref[now[4 * i + 2]])
+        buf_a[i] = near_product(sides[now[5 * i + 1]], source(now, i))
     lax.while_loop(
         lambda carry: carry[1][0] < LEAVES,
         near_body,
@@ -623,7 +679,8 @@
         out_specs=vmem,
         scratch_shapes=[
             pltpu.VMEM((LEAVES + 1, 8, LANES), F32),
-            pltpu.SMEM((LEAVES + 8,), jnp.int32),
+            pltpu.SMEM((LEAVES,), jnp.int32),
+            pltpu.SMEM((LEAVES,), jnp.int32),
             pltpu.VMEM((NEAR_UNROLL, LANES, 2 * LANES), F32),
             pltpu.VMEM((NEAR_UNROLL, LANES, 2 * LANES), F32),
         ],

time: 72.7 us -> 62.1 us (0.85)
  the two profiles are of different devices: /device:TPU:56 before, /device:TPU:6 now
where the time goes in v5:
time: 62.1 us; the launch traced here: 62 us
  Pallas kernels  62 us (100%)
    pallas_call x1, Pallas kernels, exchange(): pl.pallas_call(exchange_kernel, out_shape=(jax.ShapeDtypeStruct((LEAF_POO...  54.3 us
    pallas_call x1, Pallas kernels, field(): pl.pallas_call(field_kernel, out_shape=jax.ShapeDtypeStruct((3, LEAVES, L...  7.67 us

profile of v5, /device:TPU:6, one launch (start us, length us, event | category | flops | bytes accessed | tf_op | source)
XLA Modules:
  0.0 62.0 jit_solution(10290831509640172243)
XLA Ops:
  0.0 54.3 %exchange.1 = (f32[244,8,128]{2,1,0:T(8,128)S(1)}, bf16[64,64,256]{2,1,0:T(8,128)(2,1)S(1)}, f32[64,8,128]{2,1,0:T(8,128)S(1)}, f32[3,64,128]{2,1,0:T(8,128)S(1)}, s32[8,64]{1,0:T(8,128)S(1)}, /*index=5*/s32[64]{0:T(128)S(1)}) custom-call(f32[3,64,128]{2,1,0:T(8,128)} %bitcast.7, f32[3,64,128]{2,1,0:T(8,128)} %bitcast.8, s32[9,1,20]{2,1,0:T(1,128)} %bitcast.9, ...), custom_call_target="tpu_custom_call" | custom-call | tf_op jit(solution)/shard_map/exchange/pallas_call | solution.py:540
  54.3 7.7 %field.1 = f32[3,64,128]{2,1,0:T(8,128)} custom-call(f32[244,8,128]{2,1,0:T(8,128)S(1)} %get-tuple-element.11.pool_ref, bf16[64,64,256]{2,1,0:T(8,128)(2,1)S(1)} %get-tuple-element.12.sides, f32[64,8,128]{2,1,0:T(8,128)S(1)} %get-tuple-element.13.near0, f32[3,64,128]{2,1,0:T(8,128)S(1)} %get-tuple-element.14.far_ref, ...), custom_call_target="tpu_custom_call" | custom-call | tf_op jit(solution)/shard_map/field/pallas_call | solution.py:675

commit v6 on v5

--- a/solution.py
+++ b/solution.py
@@ -22,7 +22,13 @@
 N_DOM = 512
 NEAR_UNROLL = 8
 LEAD = 3
-HELD = (LEAVES + 6 * LEAF_SENDS, LEAVES + 7 * LEAF_SENDS)
+ENTRIES = 6 * LEAVES
+STAGES = ((0, 64, 6), (64, 32, 7), (96, 32, 8))
+DONE = STAGES[-1][0] + STAGES[-1][1]
+
+
+def held(b):
+    return LEAVES + b * LEAF_SENDS
 FAR_UNROLL = 4
 
 
@@ -255,9 +261,10 @@
 
 
 def exchange_kernel(
-    pos_in, mom_in, fl_in, fn_in, fc_in, llist_in, llen_in, clist_in, clen_in,
-    pool_ref, sides, near, far_ref, llist_out, llen_out,
+    pos_in, mom_in, fl_in, fn_in, fc_in, llist_in, llen_in, clist_in, clen_in, lens_in,
+    pool_ref, sides, near, far_ref, parts_ref, list_out,
     pos_ref, mom_ref, fl_ref, fn_ref, fc_ref, llist_ref, llen_ref, clist_ref, clen_ref, in_sem,
+    list_vec, lens_vec, key_rows, list_ref, list_sem,
     split, feats, index, cindex, gath, fsides, buf_a, buf_b, far_a, far_b, pick_a, pick_b, kept_a, kept_b,
     send_l, recv_l, send_c, recv_c, sl_sem, rl_sem, sc_sem, rc_sem,
 ):
@@ -268,7 +275,7 @@
                 (pos_in, pos_ref), (mom_in, mom_ref), (fl_in, fl_ref), (fn_in, fn_ref),
                 (fc_in, fc_ref), (llist_in, llist_ref), (llen_in, llen_ref),
                 (clist_in, clist_ref), (clen_in, clen_ref),
-                (llist_in, llist_out), (llen_in, llen_out),
+                (llist_in, list_vec), (lens_in, lens_vec),
             )
         )
     ]
@@ -369,36 +376,92 @@
             fsides[t] = far_side(pool_ref[t])
         return carry
 
-    def near_source(t, k, held):
+    def sort_list():
+        slots = list_vec[...]
+        place = iota((8, LEAVES), 0)
+        leaf = iota((8, LEAVES), 1)
+        live = (place >= 2) & (lens_vec[...] > place)
+        section = jnp.zeros((8, LEAVES), jnp.int32)
+        for b in range(SECTIONS):
+            section = section + jnp.where(slots >= held(b), 1, 0)
+        key = jnp.where(live, section, 16) * 512 + place * LEAVES + leaf
+        key = key.astype(F32)
+        for i in range(3):
+            key_rows[i : i + 1, 0:LEAVES] = key[2 + i : 3 + i]
+            key_rows[i : i + 1, LEAVES:] = key[5 + i : 6 + i]
+        source = jnp.where(live, slots + 1, 0).astype(F32)
+        both = jnp.concatenate([key, source], axis=0)
+        both = jnp.concatenate([both, jnp.zeros((16, LANES - LEAVES), F32)], axis=1)
+        turned = jnp.transpose(jnp.concatenate([both, jnp.zeros((LANES - 16, LANES), F32)], axis=0))
+        own = iota((LEAVES, LANES), 0).astype(F32)
+        spot = iota((LEAVES, LANES), 1).astype(F32)
+        got_t = [jnp.zeros((LEAVES, LANES), F32) for _ in range(3)]
+        got_s = [jnp.zeros((LEAVES, LANES), F32) for _ in range(3)]
+        for k in range(2, 8):
+            mine = jnp.broadcast_to(turned[0:LEAVES, k : k + 1], (LEAVES, LANES))
+            src = jnp.broadcast_to(turned[0:LEAVES, 8 + k : 9 + k], (LEAVES, LANES))
+            below = jnp.zeros((LEAVES, LANES), F32)
+            for i in range(3):
+                below = below + jnp.where(key_rows[i : i + 1, :] < mine, 1.0, 0.0)
+            rank = jnp.sum(below, axis=1, keepdims=True)
+            for m in range(3):
+                here = rank == spot + float(LANES * m)
+                got_t[m] = got_t[m] + jnp.where(here, own, 0.0)
+                got_s[m] = got_s[m] + jnp.where(here, src, 0.0)
+        counts = jnp.zeros((1, LANES), F32)
+        for i, b in enumerate([stage[2] for stage in STAGES] + [SECTIONS]):
+            ready = jnp.where(live & (slots < held(b)), 1.0, 0.0)
+            number = jnp.sum(jnp.sum(ready, axis=1, keepdims=True), axis=0, keepdims=True)
+            counts = jnp.where(lane[0:1] == i, number, counts)
+        list_out[...] = jnp.zeros((8, ENTRIES), jnp.int32)
+        for m in range(3):
+            cols = slice(LANES * m, LANES * m + LANES)
+            list_out[0:1, cols] = jnp.sum(got_t[m], axis=0, keepdims=True).astype(jnp.int32)
+            list_out[1:2, cols] = jnp.sum(got_s[m], axis=0, keepdims=True).astype(jnp.int32)
+        list_out[2:3, 0:LANES] = counts.astype(jnp.int32)
+
+    list_copy = pltpu.make_async_copy(list_out, list_ref, list_sem)
+
+    def near_source(t, k):
         if k == 0:
             return pool_ref[t]
-        src = llist_ref[k, t]
-        use = llen_ref[t] > k
-        if k > 1:
-            use = use & (src < held)
-        return jnp.where(use, pool_ref[src], 0.0)
-
-    def near_steps(t0, leaves, places, held=0):
-        n = len(places)
-
+        return jnp.where(llen_ref[t] > 1, pool_ref[llist_ref[1, t]], 0.0)
+
+    def near_steps(t0, leaves):
         def spot(g, i):
-            return t0 + 8 // n * g + i // n, places[i % n]
+            return t0 + 4 * g + i // 2, i % 2
 
         def first(g, i, buf):
             t, k = spot(g, i)
-            buf[i] = near_product(sides[t], near_source(t, k, held))
+            buf[i] = near_product(sides[t], near_source(t, k))
 
         def last(g, i, buf):
-            t, k = spot(g, i)
-            return near_sums(buf.at[i], near_source(t, k, held), sub)
+            return near_sums(buf.at[i], near_source(*spot(g, i)), sub)
 
         def store(g, parts):
-            for i in range(0, 8, n):
-                t, k = spot(g, i)
-                got = parts[i] if n == 1 else parts[i] + parts[i + 1]
-                near[t] = got if k == 0 else near[t] + got
-
-        near_pass(leaves * n // 8, 8, first, last, store, buf_a, buf_b)
+            for i in range(4):
+                near[t0 + 4 * g + i] = parts[2 * i] + parts[2 * i + 1]
+
+        near_pass(leaves // 4, 8, first, last, store, buf_a, buf_b)
+
+    def near_listed(n0, count, b):
+        def block(g, i):
+            src = list_ref[1, n0 + 8 * g + i]
+            use = (src > 0) & (src <= held(b))
+            return jnp.where(use, pool_ref[jnp.clip(src - 1, 0, LEAF_POOL - 1)], 0.0)
+
+        def first(g, i, buf):
+            t = jnp.clip(list_ref[0, n0 + 8 * g + i], 0, LEAVES - 1)
+            buf[i] = near_product(sides[t], block(g, i))
+
+        def last(g, i, buf):
+            return near_sums(buf.at[i], block(g, i), sub)
+
+        def store(g, parts):
+            for i in range(8):
+                parts_ref[n0 + 8 * g + i] = parts[i]
+
+        near_pass(count // 8, 8, first, last, store, buf_a, buf_b)
 
     def wanted_cells(i):
         row = cindex[pl.ds(i, 1), :]
@@ -451,23 +514,24 @@
 
     def beside(b):
         if b == 0:
+            sort_list()
+            list_copy.start()
             lax.fori_loop(0, LEAVES // 2, prepare_near, 0)
+            list_copy.wait()
         elif b == 1:
-            near_steps(0, 16, (0, 1))
+            near_steps(0, 16)
         elif b == 2:
-            near_steps(16, 16, (0, 1))
+            near_steps(16, 16)
         elif b == 3:
-            near_steps(32, 32, (0, 1))
+            near_steps(32, 32)
         elif b == 4:
             lax.fori_loop(0, LEAVES // 2, prepare_far, 0)
         elif b == 5:
             gather(0, 384)
-        elif b == 6:
-            near_steps(0, LEAVES, (2,), HELD[0])
-        elif b == 7:
-            near_steps(0, 32, (3,), HELD[1])
-        elif b == 8:
-            near_steps(32, 32, (3,), HELD[1])
+        for n0, count, when in STAGES:
+            if b == when:
+                near_listed(n0, count, b)
+        if b == SECTIONS - 1:
             gather(384, old)
 
     pl.semaphore_wait(barrier, SECTIONS)
@@ -544,10 +608,10 @@
             jax.ShapeDtypeStruct((LEAVES, 64, 2 * LANES), BF16),
             jax.ShapeDtypeStruct((LEAVES, 8, LANES), F32),
             jax.ShapeDtypeStruct((3, LEAVES, LANES), F32),
-            jax.ShapeDtypeStruct((8, LEAVES), jnp.int32),
-            jax.ShapeDtypeStruct((LEAVES,), jnp.int32),
+            jax.ShapeDtypeStruct((DONE, 8, LANES), F32),
+            jax.ShapeDtypeStruct((8, ENTRIES), jnp.int32),
         ),
-        in_specs=[hbm] * 9,
+        in_specs=[hbm] * 10,
         out_specs=(vmem,) * 6,
         scratch_shapes=[
             pltpu.VMEM((3, LEAVES, LANES), F32),
@@ -560,6 +624,11 @@
             pltpu.VMEM((LEAVES, 64), jnp.int32),
             pltpu.SMEM((LEAVES,), jnp.int32),
             pltpu.SemaphoreType.DMA((11,)),
+            pltpu.VMEM((8, LEAVES), jnp.int32),
+            pltpu.VMEM((1, LEAVES), jnp.int32),
+            pltpu.VMEM((8, LANES), F32),
+            pltpu.SMEM((8, ENTRIES), jnp.int32),
+            pltpu.SemaphoreType.DMA,
             pltpu.VMEM((48, WIDE + 64), BF16),
             pltpu.VMEM((64, WIDE + 64), BF16),
             pltpu.VMEM((16, LANES), jnp.int32),
@@ -589,115 +658,102 @@
             pltpu.with_memory_space_constraint(x, pltpu.MemorySpace.HBM)
             for x in (
                 positions, moments, fwd_leaves, fwd_counts, fwd_cells,
-                leaf_list, leaf_len, cell_list, cell_len,
+                leaf_list, leaf_len, cell_list, cell_len, leaf_len.reshape(1, LEAVES),
             )
         )
     )
 
 
 def field_kernel(
-    pool_ref, sides, near0, far_ref, llist_ref, llen_ref, out_ref, near, todo_ref, from_ref,
-    buf_a, buf_b
+    pool_ref, sides, near0, far_ref, parts_ref, list_ref, out_ref, near, more, buf_a, buf_b
 ):
     sub = iota((8, LANES), 0)
-
-    busy = jnp.int32(0)
-    for t in range(LEAVES):
-        size = llen_ref[t]
-        late = (size > 2) & (llist_ref[2, t] >= HELD[0])
-        again = (size > 3) & (llist_ref[3, t] >= HELD[1])
-        start = jnp.where(late, 2, jnp.where(again, 3, 4))
-        todo_ref[busy] = t
-        from_ref[busy] = start
-        busy = busy + (start < size).astype(jnp.int32)
-    near[0:LEAVES] = near0[...]
-
-    def near_items(at):
-        n, k = at
+    total = list_ref[2, len(STAGES)]
+    more[...] = jnp.zeros_like(more)
+
+    def add_parts(g, carry):
+        for i in range(4):
+            more[i, jnp.clip(list_ref[0, 4 * g + i], 0, LEAVES - 1)] += parts_ref[4 * g + i]
+        return carry
+
+    lax.fori_loop(0, (jnp.clip(total, 0, DONE) + 3) // 4, add_parts, 0)
+    near[0:LEAVES] = near0[...] + ((more[0] + more[1]) + (more[2] + more[3]))
+
+    def settle(n):
+        for i, (n0, count, _) in enumerate(STAGES):
+            ready = jnp.clip(list_ref[2, i] - n0, 0, count)
+            n = jnp.where(n == n0, n0 + ready, n)
+        return n
+
+    def near_items(n):
         todo = []
         for _ in range(NEAR_UNROLL):
-            here = jnp.minimum(n, LEAVES - 1)
-            t = jnp.where(n < busy, todo_ref[here], 0)
-            start = from_ref[here]
-            k = jnp.where(k < 0, jnp.where(n < busy, start, 2), k)
-            src = llist_ref[k, t]
-            used = (k != 3) | (src >= HELD[1])
-            todo += [
-                jnp.where(n < busy, t, LEAVES), t, src,
-                (k == start).astype(jnp.int32), used.astype(jnp.int32),
-            ]
-            more = k + 1 < llen_ref[t]
-            n, k = jnp.where(more, n, n + 1), jnp.where(more, k + 1, -1)
-        return (n, k), tuple(todo)
-
-    def source(todo, i):
-        return jnp.where(todo[5 * i + 4] > 0, pool_ref[todo[5 * i + 2]], 0.0)
-
-    def near_both(then, now, write, read, acc):
+            here = jnp.clip(n, 0, ENTRIES - 1)
+            t = jnp.clip(list_ref[0, here], 0, LEAVES - 1)
+            live = n < total
+            src = jnp.clip(list_ref[1, here] - 1, 0, LEAF_POOL - 1)
+            todo += [jnp.where(live, t, LEAVES), t, src]
+            n = settle(n + 1)
+        return n, tuple(todo)
+
+    def near_both(then, now, write, read):
         parts = []
         for i in range(NEAR_UNROLL):
-            write[i] = near_product(sides[then[5 * i + 1]], source(then, i))
-            parts.append(near_sums(read.at[i], source(now, i), sub))
+            write[i] = near_product(sides[then[3 * i + 1]], pool_ref[then[3 * i + 2]])
+            parts.append(near_sums(read.at[i], pool_ref[now[3 * i + 2]], sub))
         for i in range(NEAR_UNROLL):
-            acc = jnp.where(now[5 * i + 3] > 0, near0[now[5 * i + 1]], acc) + parts[i]
-            near[now[5 * i]] = acc
-        return acc
+            near[now[3 * i]] += parts[i]
 
     def near_body(carry):
-        at, now, then, acc = carry
-        at, later = near_items(at)
-        acc = near_both(then, now, buf_b, buf_a, acc)
-        at, last = near_items(at)
-        acc = near_both(later, then, buf_a, buf_b, acc)
-        return at, later, last, acc
-
-    at, now = near_items((jnp.int32(0), jnp.int32(-1)))
-    at, then = near_items(at)
-    for i in range(NEAR_UNROLL):
-        buf_a[i] = near_product(sides[now[5 * i + 1]], source(now, i))
-    lax.while_loop(
-        lambda carry: carry[1][0] < LEAVES,
-        near_body,
-        (at, now, then, jnp.zeros((8, LANES), F32)),
-    )
+        n, now, then = carry
+        n, later = near_items(n)
+        near_both(then, now, buf_b, buf_a)
+        n, last = near_items(n)
+        near_both(later, then, buf_a, buf_b)
+        return n, later, last
+
+    n, now = near_items(settle(jnp.int32(0)))
+    n, then = near_items(n)
+
+    @pl.when(now[0] < LEAVES)
+    def _():
+        for i in range(NEAR_UNROLL):
+            buf_a[i] = near_product(sides[now[3 * i + 1]], pool_ref[now[3 * i + 2]])
+        lax.while_loop(lambda carry: carry[1][0] < LEAVES, near_body, (n, now, then))
 
     for d in range(3):
-        got = near[0:LEAVES, d, :]
-        x = pool_ref[0:LEAVES, d, :]
-        out_ref[d] = (
-            3.0 * (x * near[0:LEAVES, 6, :] - got) - near[0:LEAVES, 3 + d, :] + far_ref[d]
-        )
-
-
-def field(pool, sides, near, far, leaf_list, leaf_len):
+        close = pool_ref[0:LEAVES, d, :] * near[0:LEAVES, 6, :] - near[0:LEAVES, d, :]
+        out_ref[d] = 3.0 * close - near[0:LEAVES, 3 + d, :] + far_ref[d]
+
+
+def field(pool, sides, near, far, parts, lists):
     vmem = pl.BlockSpec(memory_space=pltpu.VMEM)
     smem = pl.BlockSpec(memory_space=pltpu.SMEM)
     return pl.pallas_call(
         field_kernel,
         out_shape=jax.ShapeDtypeStruct((3, LEAVES, LANES), F32),
-        in_specs=[vmem, vmem, vmem, vmem, smem, smem],
+        in_specs=[vmem, vmem, vmem, vmem, vmem, smem],
         out_specs=vmem,
         scratch_shapes=[
             pltpu.VMEM((LEAVES + 1, 8, LANES), F32),
-            pltpu.SMEM((LEAVES,), jnp.int32),
-            pltpu.SMEM((LEAVES,), jnp.int32),
+            pltpu.VMEM((4, LEAVES, 8, LANES), F32),
             pltpu.VMEM((NEAR_UNROLL, LANES, 2 * LANES), F32),
             pltpu.VMEM((NEAR_UNROLL, LANES, 2 * LANES), F32),
         ],
         compiler_params=pltpu.CompilerParams(vmem_limit_bytes=16 * 1024 * 1024),
         name="field",
-    )(pool, sides, near, far, leaf_list, leaf_len)
+    )(pool, sides, near, far, parts, lists)
 
 
 def per_device(
     positions, moments, fwd_cells, fwd_leaves, fwd_counts, cell_list, cell_len, leaf_list, leaf_len
 ):
     swap = lambda x: jnp.transpose(x, (1, 0, 2))
-    pool, sides, near, far, lists, lens = exchange(
+    pool, sides, near, far, parts, lists = exchange(
         swap(positions), swap(moments), swap(fwd_leaves), jnp.transpose(fwd_counts, (0, 2, 1)),
         swap(fwd_cells), leaf_list.T, leaf_len, cell_list, cell_len,
     )
-    return swap(field(pool, sides, near, far, lists, lens))
+    return swap(field(pool, sides, near, far, parts, lists))
 
 
 def solution(mesh):

time: 62.1 us -> 61.2 us (0.986)
  the two profiles are of different devices: /device:TPU:6 before, /device:TPU:24 now
where the time goes in v6:
time: 61.2 us; the launch traced here: 61.1 us
  Pallas kernels  61.1 us (100%)
    pallas_call x1, Pallas kernels, exchange(): pl.pallas_call(exchange_kernel, out_shape=(jax.ShapeDtypeStruct((LEAF_POO...  54.4 us
    pallas_call x1, Pallas kernels, field(): pl.pallas_call(field_kernel, out_shape=jax.ShapeDtypeStruct((3, LEAVES, L...  6.64 us

profile of v6, /device:TPU:24, one launch (start us, length us, event | category | flops | bytes accessed | tf_op | source)
XLA Modules:
  0.0 61.1 jit_solution(4549951082406898605)
XLA Ops:
  0.0 54.4 %exchange.1 = (f32[244,8,128]{2,1,0:T(8,128)S(1)}, bf16[64,64,256]{2,1,0:T(8,128)(2,1)S(1)}, f32[64,8,128]{2,1,0:T(8,128)S(1)}, f32[3,64,128]{2,1,0:T(8,128)S(1)...) custom-call(f32[3,64,128]{2,1,0:T(8,128)} %bitcast.8, f32[3,64,128]{2,1,0:T(8,128)} %bitcast.9, s32[9,1,20]{2,1,0:T(1,128)} %bitcast.10, ...), custom_call_target="tpu_custom_call" | custom-call | tf_op jit(solution)/shard_map/exchange/pallas_call | solution.py:604
  54.5 6.6 %field.1 = f32[3,64,128]{2,1,0:T(8,128)} custom-call(f32[244,8,128]{2,1,0:T(8,128)S(1)} %get-tuple-element.11.pool_ref, bf16[64,64,256]{2,1,0:T(8,128)(2,1)S(1)} %get-tuple-element.12.sides, f32[64,8,128]{2,1,0:T(8,128)S(1)} %get-tuple-element.13.near0, f32[3,64,128]{2,1,0:T(8,128)S(1)} %get-tuple-element.14.far_ref, ...), custom_call_target="tpu_custom_call" | custom-call | tf_op jit(solution)/shard_map/field/pallas_call | solution.py:732

commit v7 on v6

--- a/solution.py
+++ b/solution.py
@@ -23,8 +23,10 @@
 NEAR_UNROLL = 8
 LEAD = 3
 ENTRIES = 6 * LEAVES
+EARLY = ((0, 32, 1), (32, 32, 2))
+EARLY_DONE = 64
 STAGES = ((0, 64, 6), (64, 32, 7), (96, 32, 8))
-DONE = STAGES[-1][0] + STAGES[-1][1]
+DONE = STAGES[-1][0] + STAGES[-1][1] + EARLY_DONE
 
 
 def held(b):
@@ -282,6 +284,8 @@
     for load in loads:
         load.start()
     me = lax.axis_index("dom")
+    core = lax.rem(me, 2)
+    base = EARLY_DONE * (1 - core)
     partners = []
     for b in range(SECTIONS):
         stride = 1 << b
@@ -409,10 +413,11 @@
                 got_t[m] = got_t[m] + jnp.where(here, own, 0.0)
                 got_s[m] = got_s[m] + jnp.where(here, src, 0.0)
         counts = jnp.zeros((1, LANES), F32)
-        for i, b in enumerate([stage[2] for stage in STAGES] + [SECTIONS]):
+        for i, b in enumerate([stage[2] for stage in EARLY + STAGES] + [SECTIONS]):
             ready = jnp.where(live & (slots < held(b)), 1.0, 0.0)
             number = jnp.sum(jnp.sum(ready, axis=1, keepdims=True), axis=0, keepdims=True)
             counts = jnp.where(lane[0:1] == i, number, counts)
+        counts = jnp.where(lane[0:1] == 6, jnp.where(core == 0, float(EARLY_DONE), 0.0), counts)
         list_out[...] = jnp.zeros((8, ENTRIES), jnp.int32)
         for m in range(3):
             cols = slice(LANES * m, LANES * m + LANES)
@@ -516,12 +521,18 @@
         if b == 0:
             sort_list()
             list_copy.start()
-            lax.fori_loop(0, LEAVES // 2, prepare_near, 0)
+            lax.fori_loop(0, LEAVES // 2 * core, prepare_near, 0)
             list_copy.wait()
-        elif b == 1:
-            near_steps(0, 16)
-        elif b == 2:
-            near_steps(16, 16)
+        elif b < 3:
+
+            @pl.when(core == 0)
+            def _():
+                near_listed(EARLY[b - 1][0], EARLY[b - 1][1], b)
+
+            @pl.when(core == 1)
+            def _():
+                near_steps(16 * (b - 1), 16)
+
         elif b == 3:
             near_steps(32, 32)
         elif b == 4:
@@ -530,9 +541,15 @@
             gather(0, 384)
         for n0, count, when in STAGES:
             if b == when:
-                near_listed(n0, count, b)
+                near_listed(base + n0, count, b)
         if b == SECTIONS - 1:
             gather(384, old)
+
+    @pl.when(core == 0)
+    def _():
+        finish_leaves(0, LEAVES)
+        lax.fori_loop(0, LEAVES // 2, prepare_near, 0)
+        near_steps(0, 32)
 
     pl.semaphore_wait(barrier, SECTIONS)
     send_leaves(0)
@@ -668,7 +685,8 @@
     pool_ref, sides, near0, far_ref, parts_ref, list_ref, out_ref, near, more, buf_a, buf_b
 ):
     sub = iota((8, LANES), 0)
-    total = list_ref[2, len(STAGES)]
+    total = list_ref[2, 5]
+    base = jnp.clip(list_ref[2, 6], 0, EARLY_DONE)
     more[...] = jnp.zeros_like(more)
 
     def add_parts(g, carry):
@@ -676,11 +694,15 @@
             more[i, jnp.clip(list_ref[0, 4 * g + i], 0, LEAVES - 1)] += parts_ref[4 * g + i]
         return carry
 
-    lax.fori_loop(0, (jnp.clip(total, 0, DONE) + 3) // 4, add_parts, 0)
+    lax.fori_loop(0, (jnp.clip(total, 0, DONE - EARLY_DONE + base) + 3) // 4, add_parts, 0)
     near[0:LEAVES] = near0[...] + ((more[0] + more[1]) + (more[2] + more[3]))
 
     def settle(n):
-        for i, (n0, count, _) in enumerate(STAGES):
+        for i, (n0, count, _) in enumerate(EARLY + STAGES):
+            if i < len(EARLY):
+                count = jnp.where(base > 0, count, 0)
+            else:
+                n0 = n0 + base
             ready = jnp.clip(list_ref[2, i] - n0, 0, count)
             n = jnp.where(n == n0, n0 + ready, n)
         return n

time: 61.2 us -> 62.1 us (1.015)
  the two profiles are of different devices: /device:TPU:24 before, /device:TPU:8 now
where the time goes in v7:
time: 62.1 us; the launch traced here: 61.8 us
  Pallas kernels  61.8 us (100%)
    pallas_call x1, Pallas kernels, exchange(): pl.pallas_call(exchange_kernel, out_shape=(jax.ShapeDtypeStruct((LEAF_POO...  57 us
    pallas_call x1, Pallas kernels, field(): pl.pallas_call(field_kernel, out_shape=jax.ShapeDtypeStruct((3, LEAVES, L...  4.76 us

profile of v7, /device:TPU:8, one launch (start us, length us, event | category | flops | bytes accessed | tf_op | source)
XLA Modules:
  0.0 61.8 jit_solution(6017633456196248236)
XLA Ops:
  0.0 57.0 %exchange.1 = (f32[244,8,128]{2,1,0:T(8,128)S(1)}, bf16[64,64,256]{2,1,0:T(8,128)(2,1)S(1)}, f32[64,8,128]{2,1,0:T(8,128)S(1)}, f32[3,64,128]{2,1,0:T(8,128)S(1)...) custom-call(f32[3,64,128]{2,1,0:T(8,128)} %bitcast.8, f32[3,64,128]{2,1,0:T(8,128)} %bitcast.9, s32[9,1,20]{2,1,0:T(1,128)} %bitcast.10, ...), custom_call_target="tpu_custom_call" | custom-call | tf_op jit(solution)/shard_map/exchange/pallas_call | solution.py:621
  57.1 4.8 %field.1 = f32[3,64,128]{2,1,0:T(8,128)} custom-call(f32[244,8,128]{2,1,0:T(8,128)S(1)} %get-tuple-element.11.pool_ref, bf16[64,64,256]{2,1,0:T(8,128)(2,1)S(1)} %get-tuple-element.12.sides, f32[64,8,128]{2,1,0:T(8,128)S(1)} %get-tuple-element.13.near0, f32[3,64,128]{2,1,0:T(8,128)S(1)} %get-tuple-element.14.far_ref, ...), custom_call_target="tpu_custom_call" | custom-call | tf_op jit(solution)/shard_map/field/pallas_call | solution.py:754
